TPU v7x, 32 devices: a whole 2x2x4 slice. The times are simulated.
32 devices in a mesh: rep: 2 (over y), exp: 16 (over z, x, core).
Axes of the slice: x: 2, y: 2, z: 4, core: 2. Of those that a mesh axis runs over, the one named last changes fastest.
Arguments:
- tokens: bfloat16 [4096, 2048], P(('rep', 'exp')), may hold values from -6 to 6
- out_grad: bfloat16 [4096, 2048], P(('rep', 'exp')), may hold values from -1.5 to 1.5
- route: int32 [4096, 4], P(('rep', 'exp')), may hold values from 0 to 15, as said below
- prob: bfloat16 [4096, 4], P(('rep', 'exp')), may hold values from 0.049804688 to 0.59765625
- w_gate: bfloat16 [16, 2048, 384], P('exp'), may hold values from -0.125 to 0.125
- w_up: bfloat16 [16, 2048, 384], P('exp'), may hold values from -0.125 to 0.125
- w_down: bfloat16 [16, 384, 2048], P('exp'), may hold values from -0.3125 to 0.3125
Outputs:
- grad_tokens: bfloat16 [4096, 2048], P(('rep', 'exp'))
- grad_prob: bfloat16 [4096, 4], P(('rep', 'exp'))
- grad_gate: bfloat16 [16, 2048, 384], P('exp', 'rep')
- grad_up: bfloat16 [16, 2048, 384], P('exp', 'rep')
- grad_down: bfloat16 [16, 384, 2048], P('exp', 'rep')
Inputs may be any that keep to these rules, and one draw needn't show every extreme that they name: `route`: each row names 4 different experts. In each aligned block of 128 rows (the rows of one device) an expert is named by at most 64 rows; one expert, the same for all blocks, is named by exactly 64 rows of every block.
All inputs are finite; a program needn't handle non-finite values.
Results may differ from a plain program's by a relative error of at most 0.0059.
Values may be sent and summed in bfloat16 or wider, within the bound.
A program may use at most 128 MiB of HBM per device.

v0:
```python
import jax
import jax.numpy as jnp
from jax import lax
from jax.sharding import PartitionSpec as P


def forward_part(input_rows, row_gradients, rows_prob, gate_weight, up_weight, down_weight):
    gate_preactivation = jnp.einsum(
        "vpc,vco->vpo", input_rows, gate_weight, preferred_element_type=jnp.float32
    )
    up_preactivation = jnp.einsum(
        "vpc,vco->vpo", input_rows, up_weight, preferred_element_type=jnp.float32
    )
    backward_rows = jnp.einsum(
        "iaj,ilj->ial", row_gradients, down_weight, preferred_element_type=jnp.float32
    )
    sigma = jax.nn.sigmoid(gate_preactivation)
    active = gate_preactivation * sigma
    hidden = active * up_preactivation
    weight_term = jnp.sum(backward_rows * hidden, axis=-1)
    weight = rows_prob.astype(jnp.float32)[..., None]
    scaled_output = (weight * hidden).astype(jnp.bfloat16)
    d_back = weight * backward_rows
    gate_gradient = (
        d_back * up_preactivation * sigma * (1.0 + gate_preactivation * (1.0 - sigma))
    ).astype(jnp.bfloat16)
    up_gradient = (d_back * active).astype(jnp.bfloat16)
    return (weight_term, scaled_output, gate_gradient, up_gradient)


def input_terms(gate_gradient, up_gradient, gate_weight, up_weight):
    leading_rows = jnp.einsum(
        "sai,sbi->sab", gate_gradient, gate_weight, preferred_element_type=jnp.float32
    )
    return leading_rows + jnp.einsum(
        "sai,sbi->sab", up_gradient, up_weight, preferred_element_type=jnp.float32
    )


def down_term(scaled_output, row_gradients):
    return jnp.einsum(
        "sub,suc->sbc", scaled_output, row_gradients, preferred_element_type=jnp.float32
    )


def gate_up_terms(input_rows, gate_gradient, up_gradient):
    gate_portion = jnp.einsum(
        "mgc,mgn->mcn", input_rows, gate_gradient, preferred_element_type=jnp.float32
    )
    up_portion = jnp.einsum(
        "mgc,mgn->mcn", input_rows, up_gradient, preferred_element_type=jnp.float32
    )
    return (gate_portion, up_portion)


def return_rows(contrib, weight_grad, target, local, topk):
    back_rows, back_prob = (
        lax.all_to_all(contrib, "exp", split_axis=1, concat_axis=0, tiled=True),
        lax.all_to_all(weight_grad, "exp", split_axis=1, concat_axis=0, tiled=True),
    )
    width = back_rows.shape[2]
    picked = back_rows.reshape(-1, width)[target].reshape(local, topk, width)
    grad_tokens = jnp.sum(picked.astype(jnp.float32), axis=1).astype(jnp.bfloat16)
    grad_prob = back_prob.reshape(-1)[target].reshape(local, topk)
    return (grad_tokens, grad_prob)


def body(tokens, out_grad, route, prob, w_gate, w_up, w_down):
    local = tokens.shape[0]
    width = tokens.shape[1]
    topk = route.shape[1]
    experts = w_gate.shape[0] * lax.axis_size("exp")
    capacity = 2 * local * topk // experts
    flat = route.reshape(-1)
    labels = jnp.arange(experts, dtype=jnp.int32)
    onehot = (flat[:, None] == labels[None, :]).astype(jnp.int32)
    earlier = jnp.cumsum(onehot, axis=0) - onehot
    position = jnp.sum(earlier * onehot, axis=1)
    target = flat * capacity + position
    source = jnp.arange(local * topk, dtype=jnp.int32) // topk
    empty_rows = jnp.zeros((experts * capacity, width), jnp.bfloat16)
    sent_rows = empty_rows.at[target].set(tokens[source]).reshape(experts, capacity, width)
    sent_grad = empty_rows.at[target].set(out_grad[source]).reshape(experts, capacity, width)
    sent_prob = (
        jnp.zeros((experts * capacity,), jnp.bfloat16)
        .at[target]
        .set(prob.reshape(-1))
        .reshape(experts, capacity)
    )
    input_rows, row_gradients, rows_prob = (
        lax.all_to_all(sent_rows, "exp", split_axis=0, concat_axis=1, tiled=True),
        lax.all_to_all(sent_grad, "exp", split_axis=0, concat_axis=1, tiled=True),
        lax.all_to_all(sent_prob, "exp", split_axis=0, concat_axis=1, tiled=True),
    )
    weight_term, scaled_output, gate_gradient, up_gradient = forward_part(
        input_rows, row_gradients, rows_prob, w_gate, w_up, w_down
    )
    down_sum = down_term(scaled_output, row_gradients)
    gate_sum, up_sum = gate_up_terms(input_rows, gate_gradient, up_gradient)
    contrib = input_terms(gate_gradient, up_gradient, w_gate, w_up).astype(jnp.bfloat16)
    grad_tokens, grad_prob = return_rows(
        contrib, weight_term.astype(jnp.bfloat16), target, local, topk
    )
    gate_mine, up_mine, down_mine = (
        lax.psum_scatter(
            gate_sum.astype(jnp.bfloat16), "rep", scatter_dimension=1, tiled=True
        ).astype(jnp.float32),
        lax.psum_scatter(
            up_sum.astype(jnp.bfloat16), "rep", scatter_dimension=1, tiled=True
        ).astype(jnp.float32),
        lax.psum_scatter(
            down_sum.astype(jnp.bfloat16), "rep", scatter_dimension=1, tiled=True
        ).astype(jnp.float32),
    )
    grad_gate = gate_mine.astype(jnp.bfloat16)
    grad_up = up_mine.astype(jnp.bfloat16)
    grad_down = down_mine.astype(jnp.bfloat16)
    return (grad_tokens, grad_prob, grad_gate, grad_up, grad_down)


def solution(mesh):
    placed = (
        P(("rep", "exp"), None),
        P(("rep", "exp"), None),
        P(("rep", "exp"), None),
        P(("rep", "exp"), None),
        P("exp", None, None),
        P("exp", None, None),
        P("exp", None, None),
    )
    return jax.shard_map(
        body,
        mesh=mesh,
        in_specs=placed,
        out_specs=(
            P(("rep", "exp"), None),
            P(("rep", "exp"), None),
            P("exp", "rep", None),
            P("exp", "rep", None),
            P("exp", "rep", None),
        ),
        check_vma=False,
    )
```

profile of v0, /device:TPU:11, one launch (start us, length us, event | category | flops | bytes accessed | tf_op | source)
XLA Modules:
  0.0 462.9 jit_solution(8866752988888304173)
XLA Ops:
  7.2 0.8 broadcast_multiply_fusion
  8.0 0.8 copy.27
  8.8 0.1 eq.29
  8.9 0.1 eq.25
  9.0 0.8 copy.30
  9.8 0.1 reshape.291
  9.9 0.1 copy.26
  10.0 0.1 mul.69
  10.2 1.2 reduce-window.6
  11.3 0.2 slice_reduce_fusion
  11.6 0.1 fusion.24
  11.7 3.8 scatter_custom_fusion
  15.5 0.7 all_to_all.20
  16.1 6.8 %all-to-all-start = ((bf16[16,1,64]{2,1,0:T(2,128)(2,1)}), bf16[16,1,64]{2,1,0:T(2,128)(2,1)S(1)}, u32[]{:S(2)}, u32[]{:S(2)}) async-start(bf16[16,1,64]{2,1,0:T(2,128)(2,1)} %all_to_all.20), calls=%async_computation | async-start | bytes 16384 | tf_op jit(solution)/shard_map/all_to_all | solution.py:93
  23.0 12.4 %scatter_custom_fusion.2 = bf16[1024,2048]{1,0:T(8,128)(2,1)} fusion(s32[512]{0:T(512)S(1)} %bitcast.75, bf16[128,2048]{1,0:T(8,128)(2,1)} %param.7, s32[1024]{0:T(1024)S(1)} %pad_clamp_fusion.1, bf16[]{:T(256)} %constant.27.clone.1), kind=kCustom, calls=%fused_computation.16 | custom fusion | bytes 4194816 | tf_op jit(solution)/shard_map/scatter | solution.py:82
  35.4 6.4 %all-to-all-start.2 = ((bf16[16,64,2048]{2,1,0:T(8,128)(2,1)}), bf16[16,64,2048]{2,1,0:T(8,128)(2,1)}, u32[]{:S(2)}, u32[]{:S(2)}) async-start(bf16[16,64,2048]{2,1,0:T(8,128)(2,1)} %bitcast.73), calls=%async_computation.2 | async-start | bytes 8388608 | tf_op jit(solution)/shard_map/all_to_all | solution.py:91
  41.8 12.6 %scatter_custom_fusion.1 = bf16[1024,2048]{1,0:T(8,128)(2,1)} fusion(s32[512]{0:T(512)S(1)} %bitcast.76, bf16[128,2048]{1,0:T(8,128)(2,1)} %param.8, s32[1024]{0:T(1024)S(1)} %pad_clamp_fusion.1, bf16[]{:T(256)} %constant.27.clone.1), kind=kCustom, calls=%fused_computation.18 | custom fusion | bytes 4194816 | tf_op jit(solution)/shard_map/scatter | solution.py:83
  54.4 79.7 %all-to-all-done.2 = bf16[16,64,2048]{2,1,0:T(8,128)(2,1)} async-done(((bf16[16,64,2048]{2,1,0:T(8,128)(2,1)}), bf16[16,64,2048]{2,1,0:T(8,128)(2,1)}, u32[]{:S(2)}, u32[]{:S(2)}) %all-to-all-start.2) | async-done | bytes 4194336 | tf_op jit(solution)/shard_map/all_to_all | solution.py:91
  134.1 4.9 %all-to-all-start.1 = ((bf16[16,64,2048]{2,1,0:T(8,128)(2,1)}), bf16[16,64,2048]{2,1,0:T(8,128)(2,1)}, u32[]{:S(2)}, u32[]{:S(2)}) async-start(bf16[16,64,2048]{2,1,0:T(8,128)(2,1)} %bitcast.72), calls=%async_computation.1 | async-start | bytes 8388608 | tf_op jit(solution)/shard_map/all_to_all | solution.py:92
  139.0 0.4 reduce-scatter.8.cloned.1.call-start
  139.5 0.1 reshape.254
  139.6 5.3 %fusion.12 = f32[1024,384]{0,1:T(8,128)} fusion(bf16[1024,2048]{1,0:T(8,128)(2,1)} %bitcast.8, bf16[1,2048,384]{2,1,0:T(8,128)(2,1)S(1)} %copy-done), kind=kOutput, calls=%fused_computation.24 | convolution fusion | flops 1610612736 | bytes 7340032 | tf_op jit(solution)/shard_map/vpc,vco->vpo/dot_general | solution.py:8
  144.9 5.2 %fusion.15 = f32[1024,384]{0,1:T(8,128)} fusion(bf16[1024,2048]{1,0:T(8,128)(2,1)} %bitcast.8, bf16[1,2048,384]{2,1,0:T(8,128)(2,1)S(1)} %copy-done.2), kind=kOutput, calls=%fused_computation.27 | convolution fusion | flops 1610612736 | bytes 7340032 | tf_op jit(solution)/shard_map/vpc,vco->vpo/dot_general | solution.py:11
  150.1 81.4 %all-to-all-done.1 = bf16[16,64,2048]{2,1,0:T(8,128)(2,1)} async-done(((bf16[16,64,2048]{2,1,0:T(8,128)(2,1)}), bf16[16,64,2048]{2,1,0:T(8,128)(2,1)}, u32[]{:S(2)}, u32[]{:S(2)}) %all-to-all-start.1) | async-done | bytes 4194336 | tf_op jit(solution)/shard_map/all_to_all | solution.py:92
  231.5 6.2 %fusion.3 = bf16[1,384,2048]{2,1,0:T(8,128)(2,1)} fusion(bf16[1024,2048]{1,0:T(8,128)(2,1)} %bitcast.5, f32[1024]{0:T(1024)S(1)} %reshape.254, f32[1024,384]{0,1:T(8,128)} %fusion.15, f32[1024,384]{0,1:T(8,128)} %fusion.12), kind=kOutput, calls=%fused_computation.15 | convolution fusion | flops 1614151680 | bytes 8916992 | tf_op jit(solution)/shard_map/sub,suc->sbc/dot_general | solution.py:41
  237.7 7.1 %multiply_reduce_fusion = (bf16[1024]{0:T(1024)(128)(2,1)S(1)}, bf16[1024,384]{0,1:T(8,128)(2,1)}, bf16[1024,384]{0,1:T(8,128)(2,1)}) fusion(f32[1024,384]{0,1:T(8,128)} %fusion.15, f32[1024,384]{0,1:T(8,128)} %fusion.12, f32[1024]{0:T(1024)S(1)} %reshape.254, bf16[1024,2048]{1,0:T(8,128)(2,1)} %bitcast.5, bf16[1,384,2048]{2,1,0:T(8,128)(2,1)} %param.13), kind=kOutput, calls=%fused_computation.32 | convolution fusion | flops 1617296384 | bytes 10491904 | tf_op jit(solution)/shard_map/iaj,ilj->ial/dot_general | solution.py:14
  244.8 0.7 convert_element_type.96
  245.5 5.1 %all-to-all-start.4 = ((bf16[1,16,64]{2,0,1:T(2,128)(2,1)}), bf16[1,16,64]{2,0,1:T(2,128)(2,1)S(1)}, u32[]{:S(2)}, u32[]{:S(2)}) async-start(bf16[1,16,64]{2,0,1:T(2,128)(2,1)} %convert_element_type.96), calls=%async_computation.4 | async-start | bytes 16384 | tf_op jit(solution)/shard_map/all_to_all | solution.py:59
  250.7 3.6 fusion.10
  254.3 2.4 fusion
  256.7 24.6 %copy.41 = bf16[1,1024,2048]{2,0,1:T(2,128)(2,1)} copy(bf16[1,1024,2048]{2,1,0:T(8,128)(2,1)S(1)} %fusion) | data formatting | bytes 8388608 | tf_op jit(solution)/shard_map/convert_element_type | solution.py:100
  281.4 0.5 broadcast.153
  281.9 26.7 %reduce.10 = bf16[1024,2048]{1,0:T(8,128)(2,1)} reduce(bf16[1024,1,2048]{2,1,0:T(2,128)(2,1)} %bitcast.70, bf16[]{:T(256)} %broadcast.153), dimensions={1}, to_apply=%bitcast.65.reduce_sub_computation | reduce | bytes 8388610
  308.6 11.4 %reshape.334 = bf16[16,2,65536]{2,1,0:T(2,128)(2,1)} reshape(bf16[1024,2048]{1,0:T(8,128)(2,1)} %reduce.10) | data formatting | bytes 8388608
  320.0 6.2 %all-to-all-start.3 = ((bf16[16,2,65536]{2,1,0:T(2,128)(2,1)}), bf16[16,2,65536]{2,1,0:T(2,128)(2,1)}, u32[]{:S(2)}, u32[]{:S(2)}) async-start(bf16[16,2,65536]{2,1,0:T(2,128)(2,1)} %reshape.334), calls=%async_computation.3 | async-start | bytes 8388608 | tf_op jit(solution)/shard_map/all_to_all | solution.py:58
  326.2 5.8 %fusion.2 = bf16[1,2048,384]{2,1,0:T(8,128)(2,1)} fusion(bf16[1024,2048]{1,0:T(8,128)(2,1)} %bitcast.8, bf16[1024,384]{0,1:T(8,128)(2,1)S(1)} %copy-done.4), kind=kOutput, calls=%fused_computation.14 | convolution fusion | flops 1611399168 | bytes 6553600 | tf_op jit(solution)/shard_map/mgc,mgn->mcn/dot_general | solution.py:50
  332.0 0.3 reduce-scatter.4.cloned.1.call-start
  332.3 5.7 %fusion.1 = bf16[1,2048,384]{2,1,0:T(8,128)(2,1)} fusion(bf16[1024,2048]{1,0:T(8,128)(2,1)} %bitcast.8, bf16[1024,384]{0,1:T(8,128)(2,1)S(1)} %copy-done.5), kind=kOutput, calls=%fused_computation.13 | convolution fusion | flops 1611399168 | bytes 6553600 | tf_op jit(solution)/shard_map/mgc,mgn->mcn/dot_general | solution.py:47
  338.1 0.1 reshape.252
  338.2 3.5 gather_fusion.1
  341.7 0.1 reshape.253
  341.8 0.7 copy.34
  342.5 76.1 %all-to-all-done.3 = bf16[16,2,65536]{2,1,0:T(2,128)(2,1)} async-done(((bf16[16,2,65536]{2,1,0:T(2,128)(2,1)}), bf16[16,2,65536]{2,1,0:T(2,128)(2,1)}, u32[]{:S(2)}, u32[]{:S(2)}) %all-to-all-start.3) | async-done | bytes 4194336 | tf_op jit(solution)/shard_map/all_to_all | solution.py:58
  418.6 12.3 %reshape.335 = bf16[1024,1,2048]{2,1,0:T(2,128)(2,1)} reshape(bf16[16,2,65536]{2,1,0:T(2,128)(2,1)} %all-to-all-done.3) | data formatting | bytes 8388608
  430.9 8.0 %copy.40 = bf16[1,1024,2048]{2,1,0:T(8,128)(2,1)} copy(bf16[1,1024,2048]{2,0,1:T(2,128)(2,1)} %bitcast.71) | data formatting | bytes 8388608
  438.9 8.0 %gather_fusion = bf16[512,2048]{1,0:T(8,128)(2,1)} fusion(bf16[1024,2048]{1,0:T(8,128)(2,1)} %bitcast.69, s32[1024]{0:T(1024)S(1)} %pad_clamp_fusion), kind=kCustom, calls=%fused_computation.2 | custom fusion | bytes 4196352 | tf_op jit(solution)/shard_map/gather | solution.py:62
  446.9 4.2 reshape.251
  451.1 5.0 %reduce_sum.34 = bf16[128,2048]{1,0:T(8,128)(2,1)} reduce(bf16[128,4,2048]{2,1,0:T(4,128)(2,1)} %reshape.251, bf16[]{:T(256)} %constant.27.clone.1), dimensions={1}, to_apply=%region_6.7 | reduce | flops 786432 | bytes 2621442 | tf_op jit(solution)/shard_map/reduce_sum | solution.py:63
  (30 shorter events, 0.3 us)
Async XLA Ops:
  7.2 132.4 %copy-start = (bf16[1,2048,384]{2,1,0:T(8,128)(2,1)S(1)}, bf16[1,2048,384]{2,1,0:T(8,128)(2,1)}, u32[]{:S(2)}) copy-start(bf16[1,2048,384]{2,1,0:T(8,128)(2,1)} %param.11) | copy-start | bytes 4718596
  16.1 19.3 %all-to-all-start = ((bf16[16,1,64]{2,1,0:T(2,128)(2,1)}), bf16[16,1,64]{2,1,0:T(2,128)(2,1)S(1)}, u32[]{:S(2)}, u32[]{:S(2)}) async-start(bf16[16,1,64]{2,1,0:T(2,128)(2,1)} %all_to_all.20), calls=%async_computation | async-start | bytes 16384 | tf_op jit(solution)/shard_map/all_to_all | solution.py:93
  35.4 98.7 %all-to-all-start.2 = ((bf16[16,64,2048]{2,1,0:T(8,128)(2,1)}), bf16[16,64,2048]{2,1,0:T(8,128)(2,1)}, u32[]{:S(2)}, u32[]{:S(2)}) async-start(bf16[16,64,2048]{2,1,0:T(8,128)(2,1)} %bitcast.73), calls=%async_computation.2 | async-start | bytes 8388608 | tf_op jit(solution)/shard_map/all_to_all | solution.py:91
  134.1 97.4 %all-to-all-start.1 = ((bf16[16,64,2048]{2,1,0:T(8,128)(2,1)}), bf16[16,64,2048]{2,1,0:T(8,128)(2,1)}, u32[]{:S(2)}, u32[]{:S(2)}) async-start(bf16[16,64,2048]{2,1,0:T(8,128)(2,1)} %bitcast.72), calls=%async_computation.1 | async-start | bytes 8388608 | tf_op jit(solution)/shard_map/all_to_all | solution.py:92
  139.0 317.1 %reduce-scatter.8.cloned.1.call-start = ((), (), s32[]{:S(2)}) async-start(), calls=%async_computation.10 | async-start | bytes 2359296 | tf_op jit(solution)/shard_map/reduce_scatter | solution.py:111
  139.6 5.3 %copy-start.2 = (bf16[1,2048,384]{2,1,0:T(8,128)(2,1)S(1)}, bf16[1,2048,384]{2,1,0:T(8,128)(2,1)}, u32[]{:S(2)}) copy-start(bf16[1,2048,384]{2,1,0:T(8,128)(2,1)} %param.12) | copy-start | bytes 4718596
  245.5 74.5 %all-to-all-start.4 = ((bf16[1,16,64]{2,0,1:T(2,128)(2,1)}), bf16[1,16,64]{2,0,1:T(2,128)(2,1)S(1)}, u32[]{:S(2)}, u32[]{:S(2)}) async-start(bf16[1,16,64]{2,0,1:T(2,128)(2,1)} %convert_element_type.96), calls=%async_computation.4 | async-start | bytes 16384 | tf_op jit(solution)/shard_map/all_to_all | solution.py:59
  250.6 3.6 copy-start.3
  319.9 6.2 %copy-start.4 = (bf16[1024,384]{0,1:T(8,128)(2,1)S(1)}, bf16[1024,384]{0,1:T(8,128)(2,1)}, u32[]{:S(2)}) copy-start(bf16[1024,384]{0,1:T(8,128)(2,1)} %get-tuple-element.22) | copy-start | bytes 2359300
  320.0 98.6 %all-to-all-start.3 = ((bf16[16,2,65536]{2,1,0:T(2,128)(2,1)}), bf16[16,2,65536]{2,1,0:T(2,128)(2,1)}, u32[]{:S(2)}, u32[]{:S(2)}) async-start(bf16[16,2,65536]{2,1,0:T(2,128)(2,1)} %reshape.334), calls=%async_computation.3 | async-start | bytes 8388608 | tf_op jit(solution)/shard_map/all_to_all | solution.py:58
  326.1 6.1 %copy-start.5 = (bf16[1024,384]{0,1:T(8,128)(2,1)S(1)}, bf16[1024,384]{0,1:T(8,128)(2,1)}, u32[]{:S(2)}) copy-start(bf16[1024,384]{0,1:T(8,128)(2,1)} %get-tuple-element.21) | copy-start | bytes 2359300
  326.1 130.0 %reduce-scatter.6.cloned.1.call-start = ((), (), s32[]{:S(2)}) async-start(), calls=%async_computation.9 | async-start | bytes 2359296 | tf_op jit(solution)/shard_map/reduce_scatter | solution.py:108
  332.0 124.1 %reduce-scatter.4.cloned.1.call-start = ((), (), s32[]{:S(2)}) async-start(), calls=%async_computation.8 | async-start | bytes 2359296 | tf_op jit(solution)/shard_map/reduce_scatter | solution.py:105
  446.9 9.2 %copy-start.1 = (bf16[1,2048,384]{2,1,0:T(8,128)(2,1)S(1)}, bf16[1,2048,384]{2,1,0:T(8,128)(2,1)}, u32[]{:S(2)}) copy-start(bf16[1,2048,384]{2,1,0:T(8,128)(2,1)} %param.11) | copy-start | bytes 4718596
Sparse Core Ops, SparseCore 0:
  237.8 25.5 reduce-scatter.7
  332.1 26.6 reduce-scatter.5
  361.7 26.0 reduce-scatter.3
where the time goes:
time: 468 us; the launch traced here: 463 us
  waiting for transfers between devices  237 us (51%)
  local copies, waits for them, and re-layouts  106 us (23%)
  matrix products  41.4 us (9%)
  other arithmetic  33.9 us (7%)
  starting transfers between devices  30.1 us (6%)
  between operations  14.2 us (3%)
    all_to_all x1, waiting for transfers between devices, body(): lax.all_to_all(sent_grad, 'exp', split_axis=0, concat_axis=1, tiled=True)  81.4 us
    all_to_all x1, waiting for transfers between devices, body(): lax.all_to_all(sent_rows, 'exp', split_axis=0, concat_axis=1, tiled=True)  79.7 us
    all_to_all x1, waiting for transfers between devices, return_rows(): lax.all_to_all(contrib, 'exp', split_axis=1, concat_axis=0, tiled=True)  76.1 us
    unnamed x19, local copies, waits for them, and re-layouts  34.5 us
    unnamed x1, other arithmetic  26.7 us
    convert_element_type x1, local copies, waits for them, and re-layouts, body(): input_terms(gate_gradient, up_gradient, w_gate, w_up).astype(jnp.bfloat16)  24.6 us
    scatter x1, local copies, waits for them, and re-layouts, body(): empty_rows.at[target].set(out_grad[source])  12.6 us
    scatter x1, local copies, waits for them, and re-layouts, body(): empty_rows.at[target].set(tokens[source]).reshape(experts, capacity, width)  12.4 us
  transfers between devices with their start and end apart: 8, of which 3 were waited for; matrix products, arithmetic and copies ran while one was open for 36% of the time, Pallas kernels for 0%

commit v1 on v0

--- a/solution.py
+++ b/solution.py
@@ -2,6 +2,9 @@
 import jax.numpy as jnp
 from jax import lax
 from jax.sharding import PartitionSpec as P
+
+F32 = jnp.float32
+BF16 = jnp.bfloat16
 
 
 def forward_part(input_rows, row_gradients, rows_prob, gate_weight, up_weight, down_weight):
@@ -53,19 +56,21 @@
     return (gate_portion, up_portion)
 
 
-def return_rows(contrib, weight_grad, target, local, topk):
+def return_rows(contrib, weight_grad, select, hits):
     back_rows, back_prob = (
         lax.all_to_all(contrib, "exp", split_axis=1, concat_axis=0, tiled=True),
         lax.all_to_all(weight_grad, "exp", split_axis=1, concat_axis=0, tiled=True),
     )
     width = back_rows.shape[2]
-    picked = back_rows.reshape(-1, width)[target].reshape(local, topk, width)
-    grad_tokens = jnp.sum(picked.astype(jnp.float32), axis=1).astype(jnp.bfloat16)
-    grad_prob = back_prob.reshape(-1)[target].reshape(local, topk)
+    grad_tokens = jnp.dot(
+        select, back_rows.reshape(-1, width), preferred_element_type=F32
+    ).astype(BF16)
+    back_prob = back_prob.reshape(-1).astype(F32)
+    grad_prob = jnp.sum(jnp.where(hits, back_prob, 0.0), axis=2).astype(BF16)
     return (grad_tokens, grad_prob)
 
 
-def body(tokens, out_grad, route, prob, w_gate, w_up, w_down):
+def routed_body(tokens, out_grad, route, prob, w_gate, w_up, w_down):
     local = tokens.shape[0]
     width = tokens.shape[1]
     topk = route.shape[1]
@@ -73,20 +78,24 @@
     capacity = 2 * local * topk // experts
     flat = route.reshape(-1)
     labels = jnp.arange(experts, dtype=jnp.int32)
-    onehot = (flat[:, None] == labels[None, :]).astype(jnp.int32)
-    earlier = jnp.cumsum(onehot, axis=0) - onehot
-    position = jnp.sum(earlier * onehot, axis=1)
+    onehot = (flat[:, None] == labels[None, :]).astype(F32)
+    order = jnp.arange(local * topk, dtype=jnp.int32)
+    before = (order[:, None] > order[None, :]).astype(BF16)
+    earlier = jnp.dot(before, onehot.astype(BF16), preferred_element_type=F32)
+    position = jnp.sum(earlier * onehot, axis=1).astype(jnp.int32)
     target = flat * capacity + position
-    source = jnp.arange(local * topk, dtype=jnp.int32) // topk
-    empty_rows = jnp.zeros((experts * capacity, width), jnp.bfloat16)
-    sent_rows = empty_rows.at[target].set(tokens[source]).reshape(experts, capacity, width)
-    sent_grad = empty_rows.at[target].set(out_grad[source]).reshape(experts, capacity, width)
-    sent_prob = (
-        jnp.zeros((experts * capacity,), jnp.bfloat16)
-        .at[target]
-        .set(prob.reshape(-1))
-        .reshape(experts, capacity)
-    )
+    slots = jnp.arange(experts * capacity, dtype=jnp.int32)
+    hits = target.reshape(local, topk)[:, :, None] == slots[None, None, :]
+    select = jnp.sum(hits.astype(F32), axis=1).astype(BF16)
+    over_rows = (((0,), (0,)), ((), ()))
+
+    def spread(rows):
+        sent = lax.dot_general(select, rows, over_rows, preferred_element_type=F32)
+        return sent.astype(BF16).reshape(experts, capacity, width)
+
+    sent_rows, sent_grad = spread(tokens), spread(out_grad)
+    sent_prob = jnp.sum(jnp.where(hits, prob.astype(F32)[:, :, None], 0.0), axis=(0, 1))
+    sent_prob = sent_prob.astype(BF16).reshape(experts, capacity)
     input_rows, row_gradients, rows_prob = (
         lax.all_to_all(sent_rows, "exp", split_axis=0, concat_axis=1, tiled=True),
         lax.all_to_all(sent_grad, "exp", split_axis=0, concat_axis=1, tiled=True),
@@ -99,7 +108,7 @@
     gate_sum, up_sum = gate_up_terms(input_rows, gate_gradient, up_gradient)
     contrib = input_terms(gate_gradient, up_gradient, w_gate, w_up).astype(jnp.bfloat16)
     grad_tokens, grad_prob = return_rows(
-        contrib, weight_term.astype(jnp.bfloat16), target, local, topk
+        contrib, weight_term.astype(jnp.bfloat16), select, hits
     )
     gate_mine, up_mine, down_mine = (
         lax.psum_scatter(
@@ -118,26 +127,65 @@
     return (grad_tokens, grad_prob, grad_gate, grad_up, grad_down)
 
 
+def gathered_body(tokens, out_grad, route, prob, w_gate, w_up, w_down):
+    local, width = tokens.shape
+    members = lax.axis_size("exp")
+    experts = w_gate.shape[0] * members
+    labels = jnp.arange(experts, dtype=jnp.int32)
+    hit = route[:, :, None] == labels[None, None, :]
+    dense = jnp.sum(jnp.where(hit, prob.astype(F32)[:, :, None], 0.0), axis=1)
+    rows = lax.all_gather(tokens, "exp", axis=0, tiled=True)
+    grads = lax.all_gather(out_grad, "exp", axis=0, tiled=True)
+    weight = lax.all_to_all(
+        dense.astype(BF16).T, "exp", split_axis=0, concat_axis=0, tiled=True
+    )
+    weight = weight.reshape(-1).astype(F32)[:, None]
+    wg, wu, wd = w_gate[0], w_up[0], w_down[0]
+    gate_pre = jnp.dot(rows, wg, preferred_element_type=F32)
+    up_pre = jnp.dot(rows, wu, preferred_element_type=F32)
+    back = lax.dot_general(grads, wd, (((1,), (1,)), ((), ())), preferred_element_type=F32)
+    sigma = jax.nn.sigmoid(gate_pre)
+    active = gate_pre * sigma
+    hidden = active * up_pre
+    term = jnp.sum(back * hidden, axis=-1).astype(BF16).reshape(members, local)
+    scaled = (weight * hidden).astype(BF16)
+    d_back = weight * back
+    d_gate = (d_back * up_pre * sigma * (1.0 + gate_pre * (1.0 - sigma))).astype(BF16)
+    d_up = (d_back * active).astype(BF16)
+    over_last = (((1,), (1,)), ((), ()))
+    contrib = lax.dot_general(d_gate, wg, over_last, preferred_element_type=F32)
+    contrib = contrib + lax.dot_general(d_up, wu, over_last, preferred_element_type=F32)
+    grad_tokens = lax.psum_scatter(
+        contrib.astype(BF16), "exp", scatter_dimension=0, tiled=True
+    )
+    over_rows = (((0,), (0,)), ((), ()))
+    parts = []
+    for left, right in ((rows, d_gate), (rows, d_up), (scaled, grads)):
+        part = lax.dot_general(left, right, over_rows, preferred_element_type=F32)
+        parts.append(
+            lax.psum_scatter(part.astype(BF16), "rep", scatter_dimension=0, tiled=True)[None]
+        )
+    term = lax.all_to_all(term, "exp", split_axis=0, concat_axis=0, tiled=True)
+    picked = jnp.where(hit, term.astype(F32).T[:, None, :], 0.0)
+    grad_prob = jnp.sum(picked, axis=2).astype(BF16)
+    return (grad_tokens, grad_prob, *parts)
+
+
+def body(tokens, out_grad, route, prob, w_gate, w_up, w_down):
+    members = lax.axis_size("exp")
+    experts = w_gate.shape[0] * members
+    plan = gathered_body if experts <= 4 * route.shape[1] else routed_body
+    return plan(tokens, out_grad, route, prob, w_gate, w_up, w_down)
+
+
 def solution(mesh):
-    placed = (
-        P(("rep", "exp"), None),
-        P(("rep", "exp"), None),
-        P(("rep", "exp"), None),
-        P(("rep", "exp"), None),
-        P("exp", None, None),
-        P("exp", None, None),
-        P("exp", None, None),
-    )
+    rows = P(("rep", "exp"), None)
+    held = P("exp", None, None)
+    halves = P("exp", "rep", None)
     return jax.shard_map(
         body,
         mesh=mesh,
-        in_specs=placed,
-        out_specs=(
-            P(("rep", "exp"), None),
-            P(("rep", "exp"), None),
-            P("exp", "rep", None),
-            P("exp", "rep", None),
-            P("exp", "rep", None),
-        ),
+        in_specs=(rows, rows, rows, rows, held, held, held),
+        out_specs=(rows, rows, halves, halves, halves),
         check_vma=False,
     )

time: 468 us -> 405 us (0.87)
  the two profiles are of different devices: /device:TPU:11 before, /device:TPU:0 now
where the time goes in v1:
time: 405 us
  waiting for transfers between devices  295 us (73%)
  matrix products  71.3 us (18%)
  between operations  14.2 us (4%)
  blocking collectives  8.97 us (2%)
  local copies, waits for them, and re-layouts  6.39 us (2%)
  other arithmetic  5.3 us (1%)
    reduce_scatter x1, waiting for transfers between devices, gathered_body(): lax.psum_scatter(contrib.astype(BF16), 'exp', scatter_dimension=0, tiled=...  110 us
    all_gather x1, waiting for transfers between devices, gathered_body(): rows = lax.all_gather(tokens, 'exp', axis=0, tiled=True)  79.1 us
    all_gather x1, waiting for transfers between devices, gathered_body(): grads = lax.all_gather(out_grad, 'exp', axis=0, tiled=True)  61.3 us
    reduce_scatter x3, waiting for transfers between devices, gathered_body(): lax.psum_scatter(part.astype(BF16), 'rep', scatter_dimension=0, tiled=True)  37.1 us
    dot_general x3, matrix products, gathered_body(): part = lax.dot_general(left, right, over_rows, preferred_element_type=F32)  25.9 us
    dot_general x1, matrix products, gathered_body(): lax.dot_general(grads, wd, (((1,), (1,)), ((), ())), preferred_element_ty...  11 us
    dot_general x1, matrix products, gathered_body(): lax.dot_general(d_up, wu, over_last, preferred_element_type=F32)  10.8 us
    dot_general x1, matrix products, gathered_body(): contrib = lax.dot_general(d_gate, wg, over_last, preferred_element_type=F32)  9.67 us
  transfers between devices with their start and end apart: 7, of which 6 were waited for; matrix products, arithmetic and copies ran while one was open for 14% of the time, Pallas kernels for 0%

profile of v1, /device:TPU:0, one launch (start us, length us, event | category | flops | bytes accessed | tf_op | source)
XLA Modules:
  0.0 405.0 jit_solution(392008216399746700)
XLA Ops:
  7.2 0.0 copy-start
  7.2 0.0 all-gather.5.cloned.1.call-start
  7.2 0.7 all-gather.5.cloned.1.call-update
  7.9 0.0 all-gather.3.cloned.1.call-start
  8.0 0.7 all-gather.3.cloned.1.call-update
  8.7 0.0 copy-start.2
  8.7 79.1 %all-gather.5.cloned.1.call-done = bf16[2048,2048]{1,0:T(8,128)(2,1)} async-done(((bf16[128,2048]{1,0:T(8,128)(2,1)}), bf16[2048,2048]{1,0:T(8,128)(2,1)}) %all-gather.5.cloned.1.call-update) | async-done | bytes 8388624 | tf_op jit(solution)/shard_map/all_gather | solution.py:137
  87.8 0.0 copy-done
  87.8 0.0 copy-start.6
  87.8 8.7 %fusion.5 = f32[2048,384]{0,1:T(8,128)} fusion(bf16[2048,2048]{1,0:T(8,128)(2,1)} %all-gather.5.cloned.1.call-done, bf16[1,2048,384]{2,1,0:T(8,128)(2,1)S(1)} %copy-done), kind=kOutput, calls=%fused_computation.14 | convolution fusion | flops 3221225472 | bytes 13107200 | tf_op jit(solution)/shard_map/dot_general | solution.py:144
  96.5 0.0 copy-done.2
  96.5 0.0 copy-done.6
  96.5 5.3 %fusion.8 = f32[2048,384]{0,1:T(8,128)} fusion(bf16[2048,2048]{1,0:T(8,128)(2,1)S(1)} %copy-done.6, bf16[1,2048,384]{2,1,0:T(8,128)(2,1)S(1)} %copy-done.2), kind=kOutput, calls=%fused_computation.17 | convolution fusion | flops 3221225472 | bytes 13107200 | tf_op jit(solution)/shard_map/dot_general | solution.py:145
  101.8 0.0 copy-start.5
  101.8 0.0 copy-start.4
  101.8 61.3 %all-gather.3.cloned.1.call-done = bf16[2048,2048]{1,0:T(8,128)(2,1)} async-done(((bf16[128,2048]{1,0:T(8,128)(2,1)}), bf16[2048,2048]{1,0:T(8,128)(2,1)}) %all-gather.3.cloned.1.call-update) | async-done | bytes 8388624 | tf_op jit(solution)/shard_map/all_gather | solution.py:138
  163.1 11.0 %multiply_reduce_fusion = (bf16[2048]{0:T(1024)(128)(2,1)S(1)}, f32[2048,384]{0,1:T(8,128)}) fusion(f32[2048,384]{0,1:T(8,128)} %fusion.8, f32[2048,384]{0,1:T(8,128)} %fusion.5, bf16[2048,2048]{1,0:T(8,128)(2,1)} %all-gather.3.cloned.1.call-done, bf16[1,384,2048]{2,1,0:T(8,128)(2,1)} %param.13), kind=kOutput, calls=%fused_computation.2 | convolution fusion | flops 3226728448 | bytes 19402752 | tf_op jit(solution)/shard_map/dot_general | solution.py:146
  174.1 0.6 copy.38
  174.7 3.5 all-to-all-start.1
  178.2 0.0 reduce-scatter.7.cloned.1.call-start
  178.2 0.0 copy-done.5
  178.3 6.2 %all-to-all-done.1 = bf16[16,1,128]{2,1,0:T(2,128)(2,1)S(1)} async-done(((bf16[16,1,128]{2,1,0:T(2,128)(2,1)}), bf16[16,1,128]{2,1,0:T(2,128)(2,1)S(1)}, u32[]{:S(2)}, u32[]{:S(2)}) %all-to-all-start.1) | async-done | bytes 4128 | tf_op jit(solution)/shard_map/all_to_all | solution.py:168
  184.5 0.0 copy-done.4
  184.5 0.6 select_reduce_fusion
  185.1 9.0 %all_to_all.15 = bf16[16,1,128]{2,1,0:T(2,128)(2,1)S(1)} all-to-all(bf16[16,1,128]{2,1,0:T(2,128)(2,1)S(1)} %copy.36), channel_id=1, replica_groups=mesh['rep'=2,'exp'=16] {'exp'}, dimensions={0} | all-to-all | bytes 8192 | tf_op jit(solution)/shard_map/all_to_all | solution.py:139
  194.1 4.7 %multiply_convert_fusion.1 = (bf16[2048,384]{0,1:T(8,128)(2,1)S(1)}, bf16[2048,384]{0,1:T(8,128)(2,1)S(1)}) fusion(f32[2048,384]{0,1:T(8,128)} %get-tuple-element.35, f32[2048]{0:T(1024)S(1)} %bitcast_convert_fusion, f32[2048,384]{0,1:T(8,128)} %fusion.5, f32[2048,384]{0,1:T(8,128)} %fusion.8), kind=kLoop, calls=%fused_computation.3 | loop fusion | flops 11010048 | bytes 12591104 | tf_op jit(solution)/shard_map/convert_element_type | solution.py:154
  198.8 0.0 copy-start.1
  198.8 1.1 copy-done.1
  199.9 7.9 %fusion.1 = bf16[2048,384]{0,1:T(8,128)(2,1)} fusion(bf16[2048,384]{0,1:T(8,128)(2,1)S(1)} %get-tuple-element.33, bf16[2048,2048]{1,0:T(8,128)(2,1)} %all-gather.5.cloned.1.call-done), kind=kOutput, calls=%fused_computation.10 | convolution fusion | flops 3222011904 | bytes 11534336 | tf_op jit(solution)/shard_map/dot_general | solution.py:164
  207.8 0.0 reduce-scatter.7.cloned.1.call-update
  207.8 0.0 reduce-scatter.9.cloned.1.call-start
  207.9 8.0 %fusion.2 = bf16[2048,384]{0,1:T(8,128)(2,1)} fusion(bf16[2048,384]{0,1:T(8,128)(2,1)S(1)} %get-tuple-element.32, bf16[2048,2048]{1,0:T(8,128)(2,1)} %all-gather.5.cloned.1.call-done), kind=kOutput, calls=%fused_computation.11 | convolution fusion | flops 3222011904 | bytes 11534336 | tf_op jit(solution)/shard_map/dot_general | solution.py:164
  215.8 0.0 reduce-scatter.9.cloned.1.call-update
  215.9 0.0 reduce-scatter.11.cloned.1.call-start
  215.9 10.1 %convolution_convert_fusion = bf16[384,2048]{1,0:T(8,128)(2,1)} fusion(bf16[2048,2048]{1,0:T(8,128)(2,1)} %all-gather.3.cloned.1.call-done, f32[2048]{0:T(1024)S(1)} %bitcast_convert_fusion, f32[2048,384]{0,1:T(8,128)} %fusion.8, f32[2048,384]{0,1:T(8,128)} %fusion.5), kind=kOutput, calls=%fused_computation.7 | convolution fusion | flops 3227516928 | bytes 16261120 | tf_op jit(solution)/shard_map/dot_general | solution.py:164
  226.0 0.0 reduce-scatter.11.cloned.1.call-update
  226.0 0.0 reduce-scatter.5.cloned.1.call-start
  226.1 0.0 copy-start.3
  226.1 9.7 %fusion.3 = f32[2048,2048]{1,0:T(8,128)} fusion(bf16[2048,384]{0,1:T(8,128)(2,1)} %copy-done.1, bf16[1,2048,384]{2,1,0:T(8,128)(2,1)S(1)} %copy-done), kind=kOutput, calls=%fused_computation.12 | convolution fusion | flops 3221225472 | bytes 19922944 | tf_op jit(solution)/shard_map/dot_general | solution.py:156
  235.7 0.0 copy-done.3
  235.7 10.8 %add_convert_fusion = bf16[2048,2048]{1,0:T(8,128)(2,1)} fusion(f32[2048,2048]{1,0:T(8,128)} %fusion.3, bf16[2048,384]{0,1:T(8,128)(2,1)S(1)} %get-tuple-element.32, bf16[1,2048,384]{2,1,0:T(8,128)(2,1)S(1)} %copy-done.3), kind=kOutput, calls=%fused_computation | convolution fusion | flops 3229614080 | bytes 28311552 | tf_op jit(solution)/shard_map/dot_general | solution.py:157
  246.6 0.0 reduce-scatter.5.cloned.1.call-update
  246.6 0.0 reduce-scatter.7.cloned.1.call-done
  246.6 2.3 copy.39
  248.9 10.7 %reduce-scatter.9.cloned.1.call-done = bf16[1024,384]{0,1:T(8,128)(2,1)} async-done(((bf16[2048,384]{0,1:T(8,128)(2,1)}), bf16[1024,384]{0,1:T(8,128)(2,1)}) %reduce-scatter.9.cloned.1.call-update) | async-done | bytes 786448 | tf_op jit(solution)/shard_map/reduce_scatter | solution.py:166
  259.6 2.3 copy.40
  261.9 26.5 %reduce-scatter.11.cloned.1.call-done = bf16[192,2048]{1,0:T(8,128)(2,1)} async-done(((bf16[384,2048]{1,0:T(8,128)(2,1)}), bf16[192,2048]{1,0:T(8,128)(2,1)}) %reduce-scatter.11.cloned.1.call-update) | async-done | bytes 786448 | tf_op jit(solution)/shard_map/reduce_scatter | solution.py:166
  288.3 109.8 %reduce-scatter.5.cloned.1.call-done = bf16[128,2048]{1,0:T(8,128)(2,1)} async-done(((bf16[2048,2048]{1,0:T(8,128)(2,1)}), bf16[128,2048]{1,0:T(8,128)(2,1)}) %reduce-scatter.5.cloned.1.call-update) | async-done | bytes 524304 | tf_op jit(solution)/shard_map/reduce_scatter | solution.py:158
  (4 shorter events, 0.0 us)
Async XLA Ops:
  7.2 80.6 %copy-start = (bf16[1,2048,384]{2,1,0:T(8,128)(2,1)S(1)}, bf16[1,2048,384]{2,1,0:T(8,128)(2,1)}, u32[]{:S(2)}) copy-start(bf16[1,2048,384]{2,1,0:T(8,128)(2,1)} %param.11) | copy-start | bytes 4718596
  7.2 80.6 %all-gather.5.cloned.1.call-start = ((), (), s32[]{:S(2)}) async-start(), calls=%async_computation.7 | async-start | bytes 8912896 | tf_op jit(solution)/shard_map/all_gather | solution.py:137
  7.9 155.2 %all-gather.3.cloned.1.call-start = ((), (), s32[]{:S(2)}) async-start(), calls=%async_computation.6 | async-start | bytes 8912896 | tf_op jit(solution)/shard_map/all_gather | solution.py:138
  8.7 87.8 %copy-start.2 = (bf16[1,2048,384]{2,1,0:T(8,128)(2,1)S(1)}, bf16[1,2048,384]{2,1,0:T(8,128)(2,1)}, u32[]{:S(2)}) copy-start(bf16[1,2048,384]{2,1,0:T(8,128)(2,1)} %param.12) | copy-start | bytes 4718596
  87.8 8.7 %copy-start.6 = (bf16[2048,2048]{1,0:T(8,128)(2,1)S(1)}, bf16[2048,2048]{1,0:T(8,128)(2,1)}, u32[]{:S(2)}) copy-start(bf16[2048,2048]{1,0:T(8,128)(2,1)} %all-gather.5.cloned.1.call-done) | copy-start | bytes 25165828
  101.8 76.4 %copy-start.5 = (bf16[128,4]{0,1:T(4,128)(2,1)S(1)}, bf16[128,4]{0,1:T(4,128)(2,1)}, u32[]{:S(2)}) copy-start(bf16[128,4]{0,1:T(4,128)(2,1)} %param.10) | copy-start | bytes 3076
  101.8 82.7 %copy-start.4 = (s32[128,4]{0,1:T(4,128)S(1)}, s32[128,4]{0,1:T(4,128)}, u32[]{:S(2)}) copy-start(s32[128,4]{0,1:T(4,128)} %param.9) | copy-start | bytes 6148
  174.7 9.8 %all-to-all-start.1 = ((bf16[16,1,128]{2,1,0:T(2,128)(2,1)}), bf16[16,1,128]{2,1,0:T(2,128)(2,1)S(1)}, u32[]{:S(2)}, u32[]{:S(2)}) async-start(bf16[16,1,128]{2,1,0:T(2,128)(2,1)} %copy.38), calls=%async_computation.2 | async-start | bytes 16384 | tf_op jit(solution)/shard_map/all_to_all | solution.py:168
  178.2 68.4 %reduce-scatter.7.cloned.1.call-start = ((), (), s32[]{:S(2)}) async-start(), calls=%async_computation.9 | async-start | bytes 2359296 | tf_op jit(solution)/shard_map/reduce_scatter | solution.py:166
  198.8 1.1 copy-start.1
  207.8 51.8 %reduce-scatter.9.cloned.1.call-start = ((), (), s32[]{:S(2)}) async-start(), calls=%async_computation.10 | async-start | bytes 2359296 | tf_op jit(solution)/shard_map/reduce_scatter | solution.py:166
  215.9 72.5 %reduce-scatter.11.cloned.1.call-start = ((), (), s32[]{:S(2)}) async-start(), calls=%async_computation.11 | async-start | bytes 2359296 | tf_op jit(solution)/shard_map/reduce_scatter | solution.py:166
  226.0 172.2 %reduce-scatter.5.cloned.1.call-start = ((), (), s32[]{:S(2)}) async-start(), calls=%async_computation.8 | async-start | bytes 8912896 | tf_op jit(solution)/shard_map/reduce_scatter | solution.py:158
  226.1 9.7 %copy-start.3 = (bf16[1,2048,384]{2,1,0:T(8,128)(2,1)S(1)}, bf16[1,2048,384]{2,1,0:T(8,128)(2,1)}, u32[]{:S(2)}) copy-start(bf16[1,2048,384]{2,1,0:T(8,128)(2,1)} %param.12) | copy-start | bytes 4718596
Sparse Core Ops, SparseCore 0:
  10.2 77.5 all-gather.4
  90.0 73.1 all-gather.2
  207.9 23.3 reduce-scatter.6
  233.5 26.0 reduce-scatter.8
  262.2 26.0 reduce-scatter.10
  293.4 104.7 reduce-scatter.4

commit v2 on v1

--- a/solution.py
+++ b/solution.py
@@ -127,48 +127,89 @@
     return (grad_tokens, grad_prob, grad_gate, grad_up, grad_down)
 
 
+def across(part, axis):
+    if lax.axis_size(axis) != 2:
+        return lax.psum_scatter(part, axis, scatter_dimension=0, tiled=True)
+    half = part.shape[0] // 2
+    me = lax.axis_index(axis)
+    theirs = lax.dynamic_slice_in_dim(part, (1 - me) * half, half, 0)
+    mine = lax.dynamic_slice_in_dim(part, me * half, half, 0)
+    arrived = lax.ppermute(theirs, axis, [(0, 1), (1, 0)])
+    return (mine.astype(F32) + arrived.astype(F32)).astype(BF16)
+
+
 def gathered_body(tokens, out_grad, route, prob, w_gate, w_up, w_down):
     local, width = tokens.shape
     members = lax.axis_size("exp")
+    chips = members // 2
     experts = w_gate.shape[0] * members
+    core = lax.rem(lax.axis_index("exp"), 2)
+    alike = [[2 * chip + c for chip in range(chips)] for c in range(2)]
+    swap = [(i, i ^ 1) for i in range(members)]
     labels = jnp.arange(experts, dtype=jnp.int32)
     hit = route[:, :, None] == labels[None, None, :]
     dense = jnp.sum(jnp.where(hit, prob.astype(F32)[:, :, None], 0.0), axis=1)
-    rows = lax.all_gather(tokens, "exp", axis=0, tiled=True)
-    grads = lax.all_gather(out_grad, "exp", axis=0, tiled=True)
     weight = lax.all_to_all(
         dense.astype(BF16).T, "exp", split_axis=0, concat_axis=0, tiled=True
-    )
-    weight = weight.reshape(-1).astype(F32)[:, None]
+    ).reshape(chips, 2, local)
+
+    def gather(rows):
+        own = lax.all_gather(rows, "exp", axis_index_groups=alike, axis=0, tiled=True)
+        return own, lax.ppermute(own, "exp", swap)
+
+    rows = gather(tokens)
+    grads = gather(out_grad)
     wg, wu, wd = w_gate[0], w_up[0], w_down[0]
-    gate_pre = jnp.dot(rows, wg, preferred_element_type=F32)
-    up_pre = jnp.dot(rows, wu, preferred_element_type=F32)
-    back = lax.dot_general(grads, wd, (((1,), (1,)), ((), ())), preferred_element_type=F32)
-    sigma = jax.nn.sigmoid(gate_pre)
-    active = gate_pre * sigma
-    hidden = active * up_pre
-    term = jnp.sum(back * hidden, axis=-1).astype(BF16).reshape(members, local)
-    scaled = (weight * hidden).astype(BF16)
-    d_back = weight * back
-    d_gate = (d_back * up_pre * sigma * (1.0 + gate_pre * (1.0 - sigma))).astype(BF16)
-    d_up = (d_back * active).astype(BF16)
     over_last = (((1,), (1,)), ((), ()))
-    contrib = lax.dot_general(d_gate, wg, over_last, preferred_element_type=F32)
-    contrib = contrib + lax.dot_general(d_up, wu, over_last, preferred_element_type=F32)
+    over_rows = (((0,), (0,)), ((), ()))
+
+    def forward(side):
+        place = core if side == 0 else 1 - core
+        prob_rows = lax.dynamic_index_in_dim(weight, place, 1, keepdims=False)
+        prob_rows = prob_rows.reshape(-1).astype(F32)[:, None]
+        gate_pre = jnp.dot(rows[side], wg, preferred_element_type=F32)
+        up_pre = jnp.dot(rows[side], wu, preferred_element_type=F32)
+        back = lax.dot_general(grads[side], wd, over_last, preferred_element_type=F32)
+        sigma = jax.nn.sigmoid(gate_pre)
+        active = gate_pre * sigma
+        hidden = active * up_pre
+        term = jnp.sum(back * hidden, axis=-1).astype(BF16).reshape(chips, local)
+        scaled = (prob_rows * hidden).astype(BF16)
+        d_back = prob_rows * back
+        slope = sigma * (1.0 + gate_pre * (1.0 - sigma))
+        d_gate = (d_back * up_pre * slope).astype(BF16)
+        d_up = (d_back * active).astype(BF16)
+        contrib = lax.dot_general(d_gate, wg, over_last, preferred_element_type=F32)
+        contrib += lax.dot_general(d_up, wu, over_last, preferred_element_type=F32)
+        return term, scaled, d_gate, d_up, contrib
+
+    far = forward(1)
+    arrived = lax.ppermute(far[4].astype(BF16), "exp", swap)
+    near = forward(0)
+    summed = (near[4] + arrived.astype(F32)).astype(BF16)
     grad_tokens = lax.psum_scatter(
-        contrib.astype(BF16), "exp", scatter_dimension=0, tiled=True
-    )
-    over_rows = (((0,), (0,)), ((), ()))
-    parts = []
-    for left, right in ((rows, d_gate), (rows, d_up), (scaled, grads)):
-        part = lax.dot_general(left, right, over_rows, preferred_element_type=F32)
-        parts.append(
-            lax.psum_scatter(part.astype(BF16), "rep", scatter_dimension=0, tiled=True)[None]
+        summed, "exp", scatter_dimension=0, axis_index_groups=alike, tiled=True
+    )
+
+    def outer(left, right):
+        total = sum(
+            lax.dot_general(a, b, over_rows, preferred_element_type=F32)
+            for a, b in zip(left, right)
         )
+        return across(total.astype(BF16), "rep")[None]
+
+    scaled, d_gate, d_up = ((near[n], far[n]) for n in (1, 2, 3))
+    grad_gate = outer(rows, d_gate)
+    grad_up = outer(rows, d_up)
+    grad_down = outer(scaled, grads)
+    flip = core == 1
+    first = jnp.where(flip, far[0], near[0])
+    second = jnp.where(flip, near[0], far[0])
+    term = jnp.stack((first, second), axis=1).reshape(members, local)
     term = lax.all_to_all(term, "exp", split_axis=0, concat_axis=0, tiled=True)
     picked = jnp.where(hit, term.astype(F32).T[:, None, :], 0.0)
     grad_prob = jnp.sum(picked, axis=2).astype(BF16)
-    return (grad_tokens, grad_prob, *parts)
+    return (grad_tokens, grad_prob, grad_gate, grad_up, grad_down)
 
 
 def body(tokens, out_grad, route, prob, w_gate, w_up, w_down):

time: 405 us -> 319 us (0.79)
  waiting for transfers between devices: 295 us -> 218 us
  matrix products: 71.3 us -> 56.1 us
  blocking collectives: 8.97 us -> 0 us
  starting transfers between devices: 3.71 us -> 10.9 us
  other arithmetic: 5.3 us -> 9.42 us
    reduce_scatter x4 -> x1, waiting for transfers between devices: 147 us -> 19.6 us  [gathered_body(): lax.psum_scatter(summed, 'exp', scatter_dimension=0, axis_index_groups=al...]
    ppermute x0 -> x6, waiting for transfers between devices: none -> 32.9 us  [the longest x3 29.1 us: across(): arrived = lax.ppermute(theirs, axis, [(0, 1), (1, 0)])]
    dot_general x8 -> x16, matrix products: 71.3 us -> 56.1 us  [the longest x6 20.5 us: outer(): lax.dot_general(a, b, over_rows, preferred_element_type=F32)]
    all_gather x2, waiting for transfers between devices: 140 us -> 151 us  [gather(): lax.all_gather(rows, 'exp', axis_index_groups=alike, axis=0, tiled=True)]
    all_to_all x1 -> x0, blocking collectives: 8.97 us -> none  [gathered_body(): lax.all_to_all(dense.astype(BF16).T, 'exp', split_axis=0, concat_axis=0,...]
    all_to_all x0 -> x1, waiting for transfers between devices: none -> 6.06 us  [gathered_body(): lax.all_to_all(dense.astype(BF16).T, 'exp', split_axis=0, concat_axis=0,...]
    broadcast_in_dim x0 -> x3, other arithmetic: none -> 4.52 us  [outer(): return across(total.astype(BF16), 'rep')[None]]
  transfers between devices with their start and end apart: 7 -> 11, of which waited for: 6 -> 9; matrix products, arithmetic and copies ran while one was open for 14% -> 16% of each run, Pallas kernels for 0% -> 0%
where the time goes in v2:
time: 319 us
  waiting for transfers between devices  218 us (68%)
  matrix products  56.1 us (18%)
  between operations  14.3 us (4%)
  starting transfers between devices  10.9 us (3%)
  local copies, waits for them, and re-layouts  10.4 us (3%)
  other arithmetic  9.42 us (3%)
    all_gather x2, waiting for transfers between devices, gather(): lax.all_gather(rows, 'exp', axis_index_groups=alike, axis=0, tiled=True)  151 us
    ppermute x3, waiting for transfers between devices, across(): arrived = lax.ppermute(theirs, axis, [(0, 1), (1, 0)])  29.1 us
    dot_general x6, matrix products, outer(): lax.dot_general(a, b, over_rows, preferred_element_type=F32)  20.5 us
    reduce_scatter x1, waiting for transfers between devices, gathered_body(): lax.psum_scatter(summed, 'exp', scatter_dimension=0, axis_index_groups=al...  19.6 us
    dot_general x2, matrix products, forward(): lax.dot_general(grads[side], wd, over_last, preferred_element_type=F32)  8.87 us
    dot_general x2, matrix products, forward(): up_pre = jnp.dot(rows[side], wu, preferred_element_type=F32)  8.66 us
    unnamed x65, local copies, waits for them, and re-layouts  7.24 us
    dot_general x2, matrix products, forward(): contrib += lax.dot_general(d_up, wu, over_last, preferred_element_type=F32)  6.84 us
  transfers between devices with their start and end apart: 11, of which 9 were waited for; matrix products, arithmetic and copies ran while one was open for 16% of the time, Pallas kernels for 0%

profile of v2, /device:TPU:0, one launch (start us, length us, event | category | flops | bytes accessed | tf_op | source)
XLA Modules:
  0.0 318.7 jit_solution(3462433884418653775)
XLA Ops:
  7.2 0.7 all-gather.5.cloned.1.call-update
  8.0 0.7 all-gather.3.cloned.1.call-update
  8.7 77.6 %all-gather.5.cloned.1.call-done = bf16[1024,2048]{1,0:T(8,128)(2,1)} async-done(((bf16[128,2048]{1,0:T(8,128)(2,1)}), bf16[1024,2048]{1,0:T(8,128)(2,1)}) %all-gather.5.cloned.1.call-update) | async-done | bytes 4194320 | tf_op jit(solution)/shard_map/all_gather | solution.py:157
  86.3 73.8 %all-gather.3.cloned.1.call-done = bf16[1024,2048]{1,0:T(8,128)(2,1)} async-done(((bf16[128,2048]{1,0:T(8,128)(2,1)}), bf16[1024,2048]{1,0:T(8,128)(2,1)}) %all-gather.3.cloned.1.call-update) | async-done | bytes 4194320 | tf_op jit(solution)/shard_map/all_gather | solution.py:157
  160.1 4.6 %fusion.14 = f32[1024,384]{0,1:T(8,128)S(1)} fusion(bf16[1024,2048]{1,0:T(8,128)(2,1)} %all-gather.5.cloned.1.call-done, bf16[1,2048,384]{2,1,0:T(8,128)(2,1)} %param.12), kind=kOutput, calls=%fused_computation.21 | convolution fusion | flops 1610612736 | bytes 7340032 | tf_op jit(solution)/shard_map/dot_general | solution.py:171
  164.8 1.8 fusion.8
  166.6 0.9 copy-done.26
  167.5 0.5 copy-done.30
  168.0 3.1 multiply_reduce_fusion
  171.1 4.0 %fusion.11 = f32[1024,384]{0,1:T(8,128)S(1)} fusion(bf16[1024,2048]{1,0:T(8,128)(2,1)} %collective-permute-done.1, bf16[1,2048,384]{2,1,0:T(8,128)(2,1)S(1)} %copy-done.2), kind=kOutput, calls=%fused_computation.18 | convolution fusion | flops 1610612736 | bytes 7340032 | tf_op jit(solution)/shard_map/dot_general | solution.py:171
  175.1 4.6 %fusion.4 = f32[1024,384]{0,1:T(8,128)S(1)} fusion(bf16[1024,2048]{1,0:T(8,128)(2,1)} %collective-permute-done.1, bf16[1,2048,384]{2,1,0:T(8,128)(2,1)S(1)} %copy-done), kind=kOutput, calls=%fused_computation.11 | convolution fusion | flops 1610612736 | bytes 7340032 | tf_op jit(solution)/shard_map/dot_general | solution.py:170
  179.8 5.8 %multiply_reduce_fusion.1 = (bf16[1024]{0:T(1024)(128)(2,1)S(1)}, f32[1024,384]{0,1:T(8,128)}) fusion(f32[1024,384]{0,1:T(8,128)S(1)} %fusion.11, f32[1024,384]{0,1:T(8,128)S(1)} %fusion.4, bf16[1024,2048]{1,0:T(8,128)(2,1)} %collective-permute-done, bf16[1,384,2048]{2,1,0:T(8,128)(2,1)S(1)} %copy-done.30), kind=kOutput, calls=%fused_computation.31 | convolution fusion | flops 1613364224 | bytes 10487808 | tf_op jit(solution)/shard_map/dot_general | solution.py:172
  185.6 0.6 copy.39
  186.2 3.5 %all-to-all-start.1 = ((bf16[16,1,128]{2,1,0:T(2,128)(2,1)}), bf16[16,1,128]{2,1,0:T(2,128)(2,1)S(1)}, u32[]{:S(2)}, u32[]{:S(2)}) async-start(bf16[16,1,128]{2,1,0:T(2,128)(2,1)} %copy.39), calls=%async_computation.2 | async-start | bytes 16384 | tf_op jit(solution)/shard_map/all_to_all | solution.py:209
  189.7 6.3 %all-to-all-done.1 = bf16[16,1,128]{2,1,0:T(2,128)(2,1)S(1)} async-done(((bf16[16,1,128]{2,1,0:T(2,128)(2,1)}), bf16[16,1,128]{2,1,0:T(2,128)(2,1)S(1)}, u32[]{:S(2)}, u32[]{:S(2)}) %all-to-all-start.1) | async-done | bytes 4128 | tf_op jit(solution)/shard_map/all_to_all | solution.py:209
  196.0 0.6 select_reduce_fusion
  196.6 0.6 copy.37
  197.2 3.5 %all-to-all-start = ((bf16[16,1,128]{2,1,0:T(2,128)(2,1)}), bf16[16,1,128]{2,1,0:T(2,128)(2,1)S(1)}, u32[]{:S(2)}, u32[]{:S(2)}) async-start(bf16[16,1,128]{2,1,0:T(2,128)(2,1)} %copy.37), calls=%async_computation | async-start | bytes 16384 | tf_op jit(solution)/shard_map/all_to_all | solution.py:152
  200.9 6.1 %all-to-all-done = bf16[16,1,128]{2,1,0:T(2,128)(2,1)S(1)} async-done(((bf16[16,1,128]{2,1,0:T(2,128)(2,1)}), bf16[16,1,128]{2,1,0:T(2,128)(2,1)S(1)}, u32[]{:S(2)}, u32[]{:S(2)}) %all-to-all-start) | async-done | bytes 4128 | tf_op jit(solution)/shard_map/all_to_all | solution.py:152
  207.0 3.3 %multiply_convert_fusion.2 = (bf16[1024,384]{0,1:T(8,128)(2,1)S(1)}, bf16[1024,384]{0,1:T(8,128)(2,1)S(1)}) fusion(f32[1024,384]{0,1:T(8,128)} %get-tuple-element.43, f32[1024]{0:T(1024)S(1)} %bitcast.89, f32[1024,384]{0,1:T(8,128)} %copy-done.21, f32[1024,384]{0,1:T(8,128)} %copy-done.19), kind=kLoop, calls=%fused_computation.32 | loop fusion | flops 5505024 | bytes 6295552 | tf_op jit(solution)/shard_map/convert_element_type | solution.py:181
  210.3 2.4 fusion.2
  212.8 2.4 add_convert_fusion.1
  215.3 1.0 multiply_convert_fusion.4
  216.3 2.4 fusion.6
  218.7 3.7 %collective-permute-done.2 = bf16[1024,2048]{1,0:T(8,128)(2,1)S(1)} collective-permute-done((bf16[1024,2048]{1,0:T(8,128)(2,1)S(1)}, bf16[1024,2048]{1,0:T(8,128)(2,1)S(1)}, u32[]{:S(2)}, u32[]{:S(2)}) %collective-permute-start.2) | collective-permute-done | bytes 4194336 | tf_op jit(solution)/shard_map/ppermute | solution.py:187
  222.4 4.4 %add_convert_fusion = bf16[1024,2048]{1,0:T(8,128)(2,1)} fusion(bf16[1024,2048]{1,0:T(8,128)(2,1)S(1)} %collective-permute-done.2, f32[1024,2048]{1,0:T(8,128)S(1)} %fusion.6, bf16[1024,384]{0,1:T(8,128)(2,1)S(1)} %get-tuple-element.32, bf16[1,2048,384]{2,1,0:T(8,128)(2,1)S(1)} %copy-done.2), kind=kOutput, calls=%fused_computation | convolution fusion | flops 1619001344 | bytes 19136512 | tf_op jit(solution)/shard_map/dot_general | solution.py:183
  226.9 1.1 copy-done.6
  228.0 4.3 %fusion.33 = f32[384,2048]{1,0:T(8,128)S(1)} fusion(bf16[1024,384]{0,1:T(8,128)(2,1)S(1)} %copy-done.6, bf16[1024,2048]{1,0:T(8,128)(2,1)} %all-gather.5.cloned.1.call-done), kind=kOutput, calls=%fused_computation.61 | convolution fusion | flops 1610612736 | bytes 8126464 | tf_op jit(solution)/shard_map/dot_general | solution.py:196
  232.3 4.2 %add_convert_fusion.3 = bf16[384,2048]{1,0:T(8,128)(2,1)S(1)} fusion(f32[384,2048]{1,0:T(8,128)S(1)} %fusion.33, bf16[1024,384]{0,1:T(8,128)(2,1)S(1)} %copy-done.4, bf16[1024,2048]{1,0:T(8,128)(2,1)} %collective-permute-done.1), kind=kOutput, calls=%fused_computation.3 | convolution fusion | flops 1612185600 | bytes 9699328 | tf_op jit(solution)/shard_map/dot_general | solution.py:196
  236.6 1.5 collective-permute-start.4
  238.1 1.8 fusion.32
  240.0 4.2 %add_convert_fusion.4 = bf16[384,2048]{1,0:T(8,128)(2,1)S(1)} fusion(f32[384,2048]{1,0:T(8,128)S(1)} %fusion.32, bf16[1024,384]{0,1:T(8,128)(2,1)S(1)} %copy-done.8, bf16[1024,2048]{1,0:T(8,128)(2,1)} %collective-permute-done.1), kind=kOutput, calls=%fused_computation.4 | convolution fusion | flops 1612185600 | bytes 9699328 | tf_op jit(solution)/shard_map/dot_general | solution.py:196
  244.2 1.2 copy-done.11
  245.3 0.9 dynamic-slice_bitcast_fusion.1
  246.3 1.0 collective-permute-start.3
  247.3 1.9 fusion.22
  249.2 4.2 %add_convert_fusion.2 = bf16[384,2048]{1,0:T(8,128)(2,1)S(1)} fusion(f32[384,2048]{1,0:T(8,128)S(1)} %fusion.22, bf16[1024,2048]{1,0:T(8,128)(2,1)} %collective-permute-done, f32[1024]{0:T(1024)S(1)} %bitcast.90, f32[1024,384]{0,1:T(8,128)S(1)} %copy-done.20, f32[1024,384]{0,1:T(8,128)S(1)} %copy-done.22), kind=kOutput, calls=%fused_computation.2 | convolution fusion | flops 1614938112 | bytes 12062720 | tf_op jit(solution)/shard_map/dot_general | solution.py:196
  253.4 1.2 copy-done.12
  254.5 0.9 constant_dynamic-slice_fusion
  255.5 1.1 collective-permute-start.5
  256.6 0.5 collective-permute-done.4
  257.3 1.2 copy.41
  258.5 15.5 %collective-permute-done.3 = bf16[1024,384]{0,1:T(8,128)(2,1)} collective-permute-done((bf16[1024,384]{0,1:T(8,128)(2,1)}, bf16[1024,384]{0,1:T(8,128)(2,1)}, u32[]{:S(2)}, u32[]{:S(2)}) %collective-permute-start.3) | collective-permute-done | bytes 786464 | tf_op jit(solution)/shard_map/ppermute | solution.py:137
  274.0 1.7 fusion.24
  275.7 1.2 copy.40
  276.9 13.2 %collective-permute-done.5 = bf16[192,2048]{1,0:T(8,128)(2,1)} collective-permute-done((bf16[192,2048]{1,0:T(8,128)(2,1)}, bf16[192,2048]{1,0:T(8,128)(2,1)}, u32[]{:S(2)}, u32[]{:S(2)}) %collective-permute-start.5) | collective-permute-done | bytes 786464 | tf_op jit(solution)/shard_map/ppermute | solution.py:137
  290.0 2.5 fusion.23
  292.6 19.6 %reduce-scatter.2.cloned.1.call-done = bf16[128,2048]{1,0:T(8,128)(2,1)} async-done(((bf16[1024,2048]{1,0:T(8,128)(2,1)}), bf16[128,2048]{1,0:T(8,128)(2,1)}) %reduce-scatter.2.cloned.1.call-update) | async-done | bytes 524304 | tf_op jit(solution)/shard_map/reduce_scatter | solution.py:190
  (75 shorter events, 1.0 us)
Async XLA Ops:
  7.2 157.6 %copy-start = (bf16[1,2048,384]{2,1,0:T(8,128)(2,1)S(1)}, bf16[1,2048,384]{2,1,0:T(8,128)(2,1)}, u32[]{:S(2)}) copy-start(bf16[1,2048,384]{2,1,0:T(8,128)(2,1)} %param.11) | copy-start | bytes 4718596
  7.2 79.1 %all-gather.5.cloned.1.call-start = ((), (), s32[]{:S(2)}) async-start(), calls=%async_computation.4 | async-start | bytes 4718592 | tf_op jit(solution)/shard_map/all_gather | solution.py:157
  7.9 152.2 %all-gather.3.cloned.1.call-start = ((), (), s32[]{:S(2)}) async-start(), calls=%async_computation.3 | async-start | bytes 4718592 | tf_op jit(solution)/shard_map/all_gather | solution.py:157
  86.3 84.8 %collective-permute-start.1 = (bf16[1024,2048]{1,0:T(8,128)(2,1)}, bf16[1024,2048]{1,0:T(8,128)(2,1)}, u32[]{:S(2)}, u32[]{:S(2)}) collective-permute-start(bf16[1024,2048]{1,0:T(8,128)(2,1)} %all-gather.5.cloned.1.call-done), channel_id=1, source_target_pairs={{0,1},{1,0},{2,3},{3,2},{4,5},{5,4},{6,7},{7,6},{8,9},{9,8},{10,11... | collective-permute-start | bytes 12582920 | tf_op jit(solution)/shard_map/ppermute | solution.py:158
  160.1 19.7 %collective-permute-start = (bf16[1024,2048]{1,0:T(8,128)(2,1)}, bf16[1024,2048]{1,0:T(8,128)(2,1)}, u32[]{:S(2)}, u32[]{:S(2)}) collective-permute-start(bf16[1024,2048]{1,0:T(8,128)(2,1)} %all-gather.3.cloned.1.call-done), channel_id=1, source_target_pairs={{0,1},{1,0},{2,3},{3,2},{4,5},{5,4},{6,7},{7,6},{8,9},{9,8},{10,11... | collective-permute-start | bytes 12582920 | tf_op jit(solution)/shard_map/ppermute | solution.py:158
  160.1 4.7 %copy-start.28 = (bf16[1024,2048]{1,0:T(8,128)(2,1)S(1)}, bf16[1024,2048]{1,0:T(8,128)(2,1)}, u32[]{:S(2)}) copy-start(bf16[1024,2048]{1,0:T(8,128)(2,1)} %all-gather.5.cloned.1.call-done) | copy-start | bytes 12582916
  164.8 1.9 copy-start.13
  164.8 2.8 copy-start.26
  164.8 3.2 %copy-start.30 = (bf16[1,384,2048]{2,1,0:T(8,128)(2,1)S(1)}, bf16[1,384,2048]{2,1,0:T(8,128)(2,1)}, u32[]{:S(2)}) copy-start(bf16[1,384,2048]{2,1,0:T(8,128)(2,1)} %param.13) | copy-start | bytes 4718596
  168.0 3.1 copy-start.16
  168.0 3.1 copy-start.2
  175.1 4.6 %copy-start.19 = (f32[1024,384]{0,1:T(8,128)}, f32[1024,384]{0,1:T(8,128)S(1)}, u32[]{:S(2)}) copy-start(f32[1024,384]{0,1:T(8,128)S(1)} %fusion.11) | copy-start | bytes 4718596
  179.7 5.9 %copy-start.21 = (f32[1024,384]{0,1:T(8,128)}, f32[1024,384]{0,1:T(8,128)S(1)}, u32[]{:S(2)}) copy-start(f32[1024,384]{0,1:T(8,128)S(1)} %fusion.4) | copy-start | bytes 4718596
  179.7 10.0 %copy-start.25 = (bf16[128,4]{0,1:T(4,128)(2,1)S(1)}, bf16[128,4]{0,1:T(4,128)(2,1)}, u32[]{:S(2)}) copy-start(bf16[128,4]{0,1:T(4,128)(2,1)} %param.10) | copy-start | bytes 3076
  179.7 16.3 %copy-start.24 = (s32[128,4]{0,1:T(4,128)S(1)}, s32[128,4]{0,1:T(4,128)}, u32[]{:S(2)}) copy-start(s32[128,4]{0,1:T(4,128)} %param.9) | copy-start | bytes 6148
  186.2 9.8 %all-to-all-start.1 = ((bf16[16,1,128]{2,1,0:T(2,128)(2,1)}), bf16[16,1,128]{2,1,0:T(2,128)(2,1)S(1)}, u32[]{:S(2)}, u32[]{:S(2)}) async-start(bf16[16,1,128]{2,1,0:T(2,128)(2,1)} %copy.39), calls=%async_computation.2 | async-start | bytes 16384 | tf_op jit(solution)/shard_map/all_to_all | solution.py:209
  197.2 9.8 %all-to-all-start = ((bf16[16,1,128]{2,1,0:T(2,128)(2,1)}), bf16[16,1,128]{2,1,0:T(2,128)(2,1)S(1)}, u32[]{:S(2)}, u32[]{:S(2)}) async-start(bf16[16,1,128]{2,1,0:T(2,128)(2,1)} %copy.37), calls=%async_computation | async-start | bytes 16384 | tf_op jit(solution)/shard_map/all_to_all | solution.py:152
  200.7 111.5 %reduce-scatter.2.cloned.1.call-start = ((), (), s32[]{:S(2)}) async-start(), calls=%async_computation.5 | async-start | bytes 4718592 | tf_op jit(solution)/shard_map/reduce_scatter | solution.py:190
  210.3 2.4 copy-start.7
  210.3 2.4 copy-start.3
  212.8 2.5 copy-start.14
  212.8 2.5 copy-start.17
  212.8 2.5 copy-start.23
  215.2 7.2 %collective-permute-start.2 = (bf16[1024,2048]{1,0:T(8,128)(2,1)S(1)}, bf16[1024,2048]{1,0:T(8,128)(2,1)S(1)}, u32[]{:S(2)}, u32[]{:S(2)}) collective-permute-start(bf16[1024,2048]{1,0:T(8,128)(2,1)S(1)} %add_convert_fusion.1), channel_id=1, source_target_pairs={{0,1},{1,0},{2,3},{3,2},{4,5},{5,4},{6,7},{7,6},{8,9},{9,8},{10,11... | collective-permute-start | bytes 12582920 | tf_op jit(solution)/shard_map/ppermute | solution.py:187
  216.3 2.4 copy-start.9
  216.3 6.1 %copy-start.5 = (bf16[1024,384]{0,1:T(8,128)(2,1)}, bf16[1024,384]{0,1:T(8,128)(2,1)S(1)}, u32[]{:S(2)}) copy-start(bf16[1024,384]{0,1:T(8,128)(2,1)S(1)} %get-tuple-element.32) | copy-start | bytes 2359300
  226.9 1.1 copy-start.6
  228.0 4.3 %copy-start.4 = (bf16[1024,384]{0,1:T(8,128)(2,1)S(1)}, bf16[1024,384]{0,1:T(8,128)(2,1)}, u32[]{:S(2)}) copy-start(bf16[1024,384]{0,1:T(8,128)(2,1)} %copy-done.3) | copy-start | bytes 2359300
  232.3 5.8 %copy-start.29 = (bf16[1024,2048]{1,0:T(8,128)(2,1)S(1)}, bf16[1024,2048]{1,0:T(8,128)(2,1)}, u32[]{:S(2)}) copy-start(bf16[1024,2048]{1,0:T(8,128)(2,1)} %all-gather.5.cloned.1.call-done) | copy-start | bytes 12582916
  236.5 1.6 copy-start.10
  236.6 3.4 %copy-start.8 = (bf16[1024,384]{0,1:T(8,128)(2,1)S(1)}, bf16[1024,384]{0,1:T(8,128)(2,1)}, u32[]{:S(2)}) copy-start(bf16[1024,384]{0,1:T(8,128)(2,1)} %copy-done.7) | copy-start | bytes 2359300
  236.6 20.4 %collective-permute-start.4 = (bf16[1024,384]{0,1:T(8,128)(2,1)S(1)}, bf16[1024,384]{0,1:T(8,128)(2,1)S(1)}, u32[]{:S(2)}, u32[]{:S(2)}) collective-permute-start(bf16[1024,384]{0,1:T(8,128)(2,1)S(1)} %dynamic-slice_bitcast_fusion), channel_id=1, source_target_pairs={{0,16},{16,0},{1,17},{17,1},{2,18},{18,2},{3,19},{19,3},{4,20},{20... | collective-permute-start | bytes 2359304 | tf_op jit(solution)/shard_map/ppermute | solution.py:137
  240.0 7.3 %copy-start.18 = (f32[1024,384]{0,1:T(8,128)S(1)}, f32[1024,384]{0,1:T(8,128)}, u32[]{:S(2)}) copy-start(f32[1024,384]{0,1:T(8,128)} %copy-done.16) | copy-start | bytes 4718596
  240.0 7.3 %copy-start.27 = (bf16[1024,2048]{1,0:T(8,128)(2,1)S(1)}, bf16[1024,2048]{1,0:T(8,128)(2,1)}, u32[]{:S(2)}) copy-start(bf16[1024,2048]{1,0:T(8,128)(2,1)} %all-gather.3.cloned.1.call-done) | copy-start | bytes 12582916
  244.2 1.2 copy-start.11
  245.3 1.9 copy-start.15
  246.3 2.9 copy-start.20
  246.3 2.9 copy-start.22
  246.3 27.7 %collective-permute-start.3 = (bf16[1024,384]{0,1:T(8,128)(2,1)}, bf16[1024,384]{0,1:T(8,128)(2,1)}, u32[]{:S(2)}, u32[]{:S(2)}) collective-permute-start(bf16[1024,384]{0,1:T(8,128)(2,1)} %dynamic-slice_bitcast_fusion.1), channel_id=1, source_target_pairs={{0,16},{16,0},{1,17},{17,1},{2,18},{18,2},{3,19},{19,3},{4,20},{20... | collective-permute-start | bytes 2359304 | tf_op jit(solution)/shard_map/ppermute | solution.py:137
  253.4 1.2 copy-start.12
  255.5 34.6 %collective-permute-start.5 = (bf16[192,2048]{1,0:T(8,128)(2,1)}, bf16[192,2048]{1,0:T(8,128)(2,1)}, u32[]{:S(2)}, u32[]{:S(2)}) collective-permute-start(bf16[192,2048]{1,0:T(8,128)(2,1)} %constant_dynamic-slice_fusion), channel_id=1, source_target_pairs={{0,16},{16,0},{1,17},{17,1},{2,18},{18,2},{3,19},{19,3},{4,20},{20... | collective-permute-start | bytes 2359304 | tf_op jit(solution)/shard_map/ppermute | solution.py:137
  275.7 36.5 %copy-start.1 = (bf16[1,2048,384]{2,1,0:T(8,128)(2,1)S(1)}, bf16[1,2048,384]{2,1,0:T(8,128)(2,1)}, u32[]{:S(2)}) copy-start(bf16[1,2048,384]{2,1,0:T(8,128)(2,1)} %param.11) | copy-start | bytes 4718596
Sparse Core Ops, SparseCore 0:
  10.1 76.0 all-gather.4
  88.4 71.6 all-gather.2
  227.0 85.1 reduce-scatter.1

commit v3 on v2

--- a/solution.py
+++ b/solution.py
@@ -144,18 +144,76 @@
     chips = members // 2
     experts = w_gate.shape[0] * members
     core = lax.rem(lax.axis_index("exp"), 2)
-    alike = [[2 * chip + c for chip in range(chips)] for c in range(2)]
+    chip = lax.axis_index("exp") // 2
+    ring = list(range(0, chips, 2)) + list(range(1, chips, 2))[::-1]
+    half = chips // 2
+    spot = jnp.where(chip % 2 == 0, chip // 2, chips - 1 - chip // 2)
+    ahead, behind = (
+        [
+            (2 * ring[p] + c, 2 * ring[(p + step) % chips] + c)
+            for p in range(chips)
+            for c in range(2)
+        ]
+        for step in (1, -1)
+    )
+    offsets = [0] + [sign * step for step in range(1, half) for sign in (-1, 1)] + [half]
+    middle = width // 2
     swap = [(i, i ^ 1) for i in range(members)]
+    sources = jnp.remainder(spot + jnp.array(offsets, jnp.int32), chips)
+    sources = jnp.where(sources < half, 2 * sources, 2 * (chips - 1 - sources) + 1)
+
+    def chosen(place):
+        ids = jnp.arange(members, dtype=jnp.int32)
+        return (2 * sources[:, None] + place == ids[None, :]).astype(BF16)
+
+    near_pick, far_pick = chosen(core), chosen(1 - core)
     labels = jnp.arange(experts, dtype=jnp.int32)
     hit = route[:, :, None] == labels[None, None, :]
     dense = jnp.sum(jnp.where(hit, prob.astype(F32)[:, :, None], 0.0), axis=1)
     weight = lax.all_to_all(
         dense.astype(BF16).T, "exp", split_axis=0, concat_axis=0, tiled=True
-    ).reshape(chips, 2, local)
+    ).reshape(members, local)
 
     def gather(rows):
-        own = lax.all_gather(rows, "exp", axis_index_groups=alike, axis=0, tiled=True)
+        blocks = [rows]
+        right = left = rows
+        for _ in range(1, half):
+            right = lax.ppermute(right, "exp", ahead)
+            left = lax.ppermute(left, "exp", behind)
+            blocks += [right, left]
+        blocks.append(
+            jnp.concatenate(
+                (
+                    lax.ppermute(right[:, :middle], "exp", ahead),
+                    lax.ppermute(left[:, middle:], "exp", behind),
+                ),
+                axis=1,
+            )
+        )
+        own = jnp.concatenate(blocks, axis=0)
         return own, lax.ppermute(own, "exp", swap)
+
+    def give_back(terms):
+        def term(offset):
+            at = offsets.index(offset) * local
+            return terms[at : at + local]
+
+        def add(held, arrived):
+            return (held.astype(F32) + arrived.astype(F32)).astype(BF16)
+
+        right = lax.ppermute(term(half)[:, :middle], "exp", ahead)
+        left = lax.ppermute(term(half)[:, middle:], "exp", behind)
+        for step in range(half - 1, 0, -1):
+            held, other = term(step), term(-step)
+            if step == half - 1:
+                right = jnp.concatenate((add(held[:, :middle], right), held[:, middle:]), axis=1)
+                left = jnp.concatenate((other[:, :middle], add(other[:, middle:], left)), axis=1)
+            else:
+                right, left = add(held, right), add(other, left)
+            right = lax.ppermute(right, "exp", ahead)
+            left = lax.ppermute(left, "exp", behind)
+        total = term(0).astype(F32) + right.astype(F32) + left.astype(F32)
+        return total.astype(BF16)
 
     rows = gather(tokens)
     grads = gather(out_grad)
@@ -164,9 +222,8 @@
     over_rows = (((0,), (0,)), ((), ()))
 
     def forward(side):
-        place = core if side == 0 else 1 - core
-        prob_rows = lax.dynamic_index_in_dim(weight, place, 1, keepdims=False)
-        prob_rows = prob_rows.reshape(-1).astype(F32)[:, None]
+        pick = near_pick if side == 0 else far_pick
+        prob_rows = jnp.dot(pick, weight, preferred_element_type=F32).reshape(-1)[:, None]
         gate_pre = jnp.dot(rows[side], wg, preferred_element_type=F32)
         up_pre = jnp.dot(rows[side], wu, preferred_element_type=F32)
         back = lax.dot_general(grads[side], wd, over_last, preferred_element_type=F32)
@@ -187,9 +244,7 @@
     arrived = lax.ppermute(far[4].astype(BF16), "exp", swap)
     near = forward(0)
     summed = (near[4] + arrived.astype(F32)).astype(BF16)
-    grad_tokens = lax.psum_scatter(
-        summed, "exp", scatter_dimension=0, axis_index_groups=alike, tiled=True
-    )
+    grad_tokens = give_back(summed)
 
     def outer(left, right):
         total = sum(
@@ -202,10 +257,9 @@
     grad_gate = outer(rows, d_gate)
     grad_up = outer(rows, d_up)
     grad_down = outer(scaled, grads)
-    flip = core == 1
-    first = jnp.where(flip, far[0], near[0])
-    second = jnp.where(flip, near[0], far[0])
-    term = jnp.stack((first, second), axis=1).reshape(members, local)
+    term = lax.dot_general(near_pick, near[0], over_rows, preferred_element_type=F32)
+    term += lax.dot_general(far_pick, far[0], over_rows, preferred_element_type=F32)
+    term = term.astype(BF16)
     term = lax.all_to_all(term, "exp", split_axis=0, concat_axis=0, tiled=True)
     picked = jnp.where(hit, term.astype(F32).T[:, None, :], 0.0)
     grad_prob = jnp.sum(picked, axis=2).astype(BF16)
@@ -215,7 +269,8 @@
 def body(tokens, out_grad, route, prob, w_gate, w_up, w_down):
     members = lax.axis_size("exp")
     experts = w_gate.shape[0] * members
-    plan = gathered_body if experts <= 4 * route.shape[1] else routed_body
+    near = experts <= 4 * route.shape[1] and members >= 8 and members % 4 == 0
+    plan = gathered_body if near else routed_body
     return plan(tokens, out_grad, route, prob, w_gate, w_up, w_down)
 
 

time: 319 us -> 256 us (0.80)
  waiting for transfers between devices: 218 us -> 106 us
  starting transfers between devices: 10.9 us -> 34.8 us
  matrix products: 56.1 us -> 72.4 us
  between operations: 14.3 us -> 1.43 us
  blocking collectives: 0 us -> 8.97 us
  other arithmetic: 9.42 us -> 14.2 us
  local copies, waits for them, and re-layouts: 10.4 us -> 15.1 us
    all_gather x2 -> x0, waiting for transfers between devices: 151 us -> none  [gather(): lax.all_gather(rows, 'exp', axis_index_groups=alike, axis=0, tiled=True)]
    ppermute x0 -> x24, waiting for transfers between devices: none -> 79 us  [the longest x6 38.1 us: gather(): right = lax.ppermute(right, 'exp', ahead)]
    ppermute x0 -> x24, starting transfers between devices: none -> 27.1 us  [the longest x6 13.7 us: gather(): right = lax.ppermute(right, 'exp', ahead)]
    reduce_scatter x1 -> x0, waiting for transfers between devices: 19.6 us -> none  [gathered_body(): lax.psum_scatter(summed, 'exp', scatter_dimension=0, axis_index_groups=al...]
    all_to_all x0 -> x1, blocking collectives: none -> 8.97 us  [gathered_body(): lax.all_to_all(dense.astype(BF16).T, 'exp', split_axis=0, concat_axis=0,...]
    ppermute x3, waiting for transfers between devices: 29.1 us -> 20.5 us  [across(): arrived = lax.ppermute(theirs, axis, [(0, 1), (1, 0)])]
    dot_general x6, matrix products: 20.5 us -> 28.7 us  [outer(): lax.dot_general(a, b, over_rows, preferred_element_type=F32)]
    unnamed x65 -> x54, local copies, waits for them, and re-layouts: 7.24 us -> 14.1 us
  transfers between devices with their start and end apart: 11 -> 31, of which waited for: 9 -> 17; matrix products, arithmetic and copies ran while one was open for 16% -> 31% of each run, Pallas kernels for 0% -> 0%
where the time goes in v3:
time: 256 us; the launch traced here: 253 us
  waiting for transfers between devices  106 us (41%)
  matrix products  72.4 us (28%)
  starting transfers between devices  34.8 us (14%)
  local copies, waits for them, and re-layouts  15.1 us (6%)
  other arithmetic  14.2 us (6%)
  blocking collectives  8.97 us (4%)
    ppermute x6, waiting for transfers between devices, gather(): right = lax.ppermute(right, 'exp', ahead)  38.1 us
    dot_general x6, matrix products, outer(): lax.dot_general(a, b, over_rows, preferred_element_type=F32)  28.7 us
    ppermute x3, waiting for transfers between devices, across(): arrived = lax.ppermute(theirs, axis, [(0, 1), (1, 0)])  20.5 us
    ppermute x2, waiting for transfers between devices, gather(): lax.ppermute(right[:, :middle], 'exp', ahead)  16.4 us
    unnamed x54, local copies, waits for them, and re-layouts  14.1 us
    ppermute x3, waiting for transfers between devices, give_back(): right = lax.ppermute(right, 'exp', ahead)  13.8 us
    ppermute x6, starting transfers between devices, gather(): right = lax.ppermute(right, 'exp', ahead)  13.7 us
    dot_general x2, matrix products, forward(): lax.dot_general(grads[side], wd, over_last, preferred_element_type=F32)  11.6 us
  transfers between devices with their start and end apart: 31, of which 17 were waited for; matrix products, arithmetic and copies ran while one was open for 31% of the time, Pallas kernels for 0%

profile of v3, /device:TPU:0, one launch (start us, length us, event | category | flops | bytes accessed | tf_op | source)
XLA Modules:
  0.0 252.9 jit_solution(6759239206121792930)
XLA Ops:
  0.6 3.1 %collective-permute-start.8 = (bf16[128,2048]{1,0:T(8,128)(2,1)}, bf16[128,2048]{1,0:T(8,128)(2,1)S(1)}, u32[]{:S(2)}, u32[]{:S(2)}) collective-permute-start(bf16[128,2048]{1,0:T(8,128)(2,1)} %param.8), channel_id=1, source_target_pairs={{0,4},{1,5},{4,8},{5,9},{8,12},{9,13},{12,14},{13,15},{14,10},{15,... | collective-permute-start | bytes 1572872 | tf_op jit(solution)/shard_map/ppermute | solution.py:181
  3.7 2.0 collective-permute-start
  5.8 1.9 constant_dynamic-update-slice_fusion.13
  7.7 1.9 constant_dynamic-update-slice_fusion.6
  9.5 7.1 %collective-permute-done.8 = bf16[128,2048]{1,0:T(8,128)(2,1)S(1)} collective-permute-done((bf16[128,2048]{1,0:T(8,128)(2,1)}, bf16[128,2048]{1,0:T(8,128)(2,1)S(1)}, u32[]{:S(2)}, u32[]{:S(2)}) %collective-permute-start.8) | collective-permute-done | bytes 524320 | tf_op jit(solution)/shard_map/ppermute | solution.py:181
  16.6 2.1 collective-permute-start.10
  19.7 8.2 %collective-permute-done = bf16[128,2048]{1,0:T(8,128)(2,1)S(1)} collective-permute-done((bf16[128,2048]{1,0:T(8,128)(2,1)}, bf16[128,2048]{1,0:T(8,128)(2,1)S(1)}, u32[]{:S(2)}, u32[]{:S(2)}) %collective-permute-start) | collective-permute-done | bytes 524320 | tf_op jit(solution)/shard_map/ppermute | solution.py:181
  27.8 2.1 collective-permute-start.2
  31.7 7.3 %collective-permute-done.10 = bf16[128,2048]{1,0:T(8,128)(2,1)S(1)} collective-permute-done((bf16[128,2048]{1,0:T(8,128)(2,1)S(1)}, bf16[128,2048]{1,0:T(8,128)(2,1)S(1)}, u32[]{:S(2)}, u32[]{:S(2)}) %collective-permute-start.10) | collective-permute-done | bytes 524320 | tf_op jit(solution)/shard_map/ppermute | solution.py:181
  39.1 2.1 collective-permute-start.12
  42.1 8.2 %collective-permute-done.2 = bf16[128,2048]{1,0:T(8,128)(2,1)S(1)} collective-permute-done((bf16[128,2048]{1,0:T(8,128)(2,1)S(1)}, bf16[128,2048]{1,0:T(8,128)(2,1)S(1)}, u32[]{:S(2)}, u32[]{:S(2)}) %collective-permute-start.2) | collective-permute-done | bytes 524320 | tf_op jit(solution)/shard_map/ppermute | solution.py:181
  50.3 2.1 collective-permute-start.4
  54.2 7.4 %collective-permute-done.12 = bf16[128,2048]{1,0:T(8,128)(2,1)S(1)} collective-permute-done((bf16[128,2048]{1,0:T(8,128)(2,1)S(1)}, bf16[128,2048]{1,0:T(8,128)(2,1)S(1)}, u32[]{:S(2)}, u32[]{:S(2)}) %collective-permute-start.12) | collective-permute-done | bytes 524320 | tf_op jit(solution)/shard_map/ppermute | solution.py:181
  61.6 2.2 collective-permute-start.14
  65.6 12.0 %collective-permute-done.14 = bf16[128,1024]{1,0:T(8,128)(2,1)S(1)} collective-permute-done((bf16[128,1024]{1,0:T(8,128)(2,1)S(1)}, bf16[128,1024]{1,0:T(8,128)(2,1)S(1)}, u32[]{:S(2)}, u32[]{:S(2)}) %collective-permute-start.14) | collective-permute-done | bytes 262176 | tf_op jit(solution)/shard_map/ppermute | solution.py:187
  77.6 1.5 collective-permute-done.15
  81.7 1.6 collective-permute-start.6
  86.1 4.4 %collective-permute-done.6 = bf16[128,1024]{1,0:T(8,128)(2,1)S(1)} collective-permute-done((bf16[128,1024]{1,0:T(8,128)(2,1)S(1)}, bf16[128,1024]{1,0:T(8,128)(2,1)S(1)}, u32[]{:S(2)}, u32[]{:S(2)}) %collective-permute-start.6) | collective-permute-done | bytes 262176 | tf_op jit(solution)/shard_map/ppermute | solution.py:187
  90.5 1.9 collective-permute-done.7
  93.3 4.0 %fusion.12 = f32[1024,384]{0,1:T(8,128)S(1)} fusion(bf16[1024,2048]{1,0:T(8,128)(2,1)} %maximum_dynamic-update-slice_fusion.1, bf16[1,2048,384]{2,1,0:T(8,128)(2,1)S(1)} %copy-done.2), kind=kOutput, calls=%fused_computation.17 | convolution fusion | flops 1610612736 | bytes 7340032 | tf_op jit(solution)/shard_map/dot_general | solution.py:228
  97.4 4.6 %fusion.6 = f32[1024,384]{0,1:T(8,128)S(1)} fusion(bf16[1024,2048]{1,0:T(8,128)(2,1)} %maximum_dynamic-update-slice_fusion.1, bf16[1,2048,384]{2,1,0:T(8,128)(2,1)S(1)} %copy-done), kind=kOutput, calls=%fused_computation.11 | convolution fusion | flops 1610612736 | bytes 7340032 | tf_op jit(solution)/shard_map/dot_general | solution.py:227
  102.0 5.8 %multiply_reduce_fusion.1 = (bf16[1024]{0:T(1024)(128)(2,1)S(1)}, f32[1024,384]{0,1:T(8,128)}) fusion(f32[1024,384]{0,1:T(8,128)S(1)} %fusion.12, f32[1024,384]{0,1:T(8,128)S(1)} %fusion.6, bf16[1024,2048]{1,0:T(8,128)(2,1)} %maximum_dynamic-update-slice_fusion, bf16[1,384,2048]{2,1,0:T(8,128)(2,1)S(1)} %copy-done.18), kind=kOutput, calls=%fused_computation.29 | convolution fusion | flops 1613364224 | bytes 10487808 | tf_op jit(solution)/shard_map/dot_general | solution.py:229
  108.1 4.0 %fusion.2 = f32[1024,384]{0,1:T(8,128)S(1)} fusion(bf16[1024,2048]{1,0:T(8,128)(2,1)} %collective-permute-done.17, bf16[1,2048,384]{2,1,0:T(8,128)(2,1)S(1)} %copy-done), kind=kOutput, calls=%fused_computation.7 | convolution fusion | flops 1610612736 | bytes 7340032 | tf_op jit(solution)/shard_map/dot_general | solution.py:227
  112.1 4.6 %fusion.9 = f32[1024,384]{0,1:T(8,128)S(1)} fusion(bf16[1024,2048]{1,0:T(8,128)(2,1)} %collective-permute-done.17, bf16[1,2048,384]{2,1,0:T(8,128)(2,1)S(1)} %copy-done.2), kind=kOutput, calls=%fused_computation.14 | convolution fusion | flops 1610612736 | bytes 7340032 | tf_op jit(solution)/shard_map/dot_general | solution.py:228
  116.8 5.8 %multiply_reduce_fusion = (bf16[1024]{0:T(1024)(128)(2,1)S(1)}, f32[1024,384]{0,1:T(8,128)}) fusion(f32[1024,384]{0,1:T(8,128)S(1)} %fusion.9, f32[1024,384]{0,1:T(8,128)S(1)} %fusion.2, bf16[1024,2048]{1,0:T(8,128)(2,1)} %collective-permute-done.16, bf16[1,384,2048]{2,1,0:T(8,128)(2,1)S(1)} %copy-done.18), kind=kOutput, calls=%fused_computation.28 | convolution fusion | flops 1613364224 | bytes 10487808 | tf_op jit(solution)/shard_map/dot_general | solution.py:229
  123.4 4.0 %all-to-all-start.1 = ((bf16[16,1,128]{2,1,0:T(2,128)(2,1)}), bf16[16,1,128]{2,1,0:T(2,128)(2,1)S(1)}, u32[]{:S(2)}, u32[]{:S(2)}) async-start(bf16[16,1,128]{2,1,0:T(2,128)(2,1)} %copy.26), calls=%async_computation.1 | async-start | bytes 16384 | tf_op jit(solution)/shard_map/all_to_all | solution.py:263
  127.4 6.3 %all-to-all-done.1 = bf16[16,1,128]{2,1,0:T(2,128)(2,1)S(1)} async-done(((bf16[16,1,128]{2,1,0:T(2,128)(2,1)}), bf16[16,1,128]{2,1,0:T(2,128)(2,1)S(1)}, u32[]{:S(2)}, u32[]{:S(2)}) %all-to-all-start.1) | async-done | bytes 4128 | tf_op jit(solution)/shard_map/all_to_all | solution.py:263
  134.3 9.0 %all_to_all.21 = bf16[16,1,128]{2,1,0:T(2,128)(2,1)S(1)} all-to-all(bf16[16,1,128]{2,1,0:T(2,128)(2,1)S(1)} %copy.25), channel_id=1, replica_groups=mesh['rep'=2,'exp'=16] {'exp'}, dimensions={0} | all-to-all | bytes 8192 | tf_op jit(solution)/shard_map/all_to_all | solution.py:173
  143.5 3.3 %multiply_convert_fusion.2 = (bf16[1024,384]{0,1:T(8,128)(2,1)S(1)}, bf16[1024,384]{0,1:T(8,128)(2,1)S(1)}) fusion(f32[1024,384]{0,1:T(8,128)} %get-tuple-element.24, f32[1024]{0:T(1024)S(1)} %convolution_bitcast_fusion, f32[1024,384]{0,1:T(8,128)} %copy-done.11, f32[1024,384]{0,1:T(8,128)} %copy-done.13), kind=kLoop, calls=%fused_computation.30 | loop fusion | flops 5505024 | bytes 6295552 | tf_op jit(solution)/shard_map/convert_element_type | solution.py:238
  146.8 2.4 fusion
  149.3 4.5 %add_convert_fusion.1 = bf16[1024,2048]{1,0:T(8,128)(2,1)} fusion(f32[1024,2048]{1,0:T(8,128)S(1)} %fusion, bf16[1024,384]{0,1:T(8,128)(2,1)S(1)} %get-tuple-element.19, bf16[1,2048,384]{2,1,0:T(8,128)(2,1)S(1)} %copy-done.2), kind=kOutput, calls=%fused_computation.1 | convolution fusion | flops 1614807040 | bytes 14942208 | tf_op jit(solution)/shard_map/dot_general | solution.py:240
  154.0 3.3 %multiply_convert_fusion.4 = (bf16[1024,384]{0,1:T(8,128)(2,1)S(1)}, bf16[1024,384]{0,1:T(8,128)(2,1)S(1)}) fusion(f32[1024,384]{0,1:T(8,128)} %get-tuple-element.22, f32[1024]{0:T(1024)S(1)} %convolution_bitcast_fusion.1, f32[1024,384]{0,1:T(8,128)} %copy-done.9, f32[1024,384]{0,1:T(8,128)} %copy-done.7), kind=kLoop, calls=%fused_computation.34 | loop fusion | flops 5505024 | bytes 6295552 | tf_op jit(solution)/shard_map/convert_element_type | solution.py:238
  157.3 2.4 fusion.4
  159.7 6.4 %fusion.50 = f32[2048,384]{1,0:T(8,128)} fusion(bf16[1024,2048]{1,0:T(8,128)(2,1)} %collective-permute-done.17, bf16[1024,384]{0,1:T(8,128)(2,1)S(1)} %copy-done.4), kind=kOutput, calls=%fused_computation.108 | convolution fusion | flops 1610612736 | bytes 8126464 | tf_op jit(solution)/shard_map/dot_general | solution.py:251
  166.1 4.4 %fusion.24 = f32[384,2048]{1,0:T(8,128)S(1)} fusion(bf16[1024,2048]{1,0:T(8,128)(2,1)} %collective-permute-done.16, f32[1024]{0:T(1024)S(1)} %convolution_bitcast_fusion, f32[1024,384]{0,1:T(8,128)S(1)} %copy-done.14, f32[1024,384]{0,1:T(8,128)S(1)} %copy-done.12), kind=kOutput, calls=%fused_computation.50 | convolution fusion | flops 1613365248 | bytes 10489856 | tf_op jit(solution)/shard_map/dot_general | solution.py:251
  170.5 4.0 %add_convert_fusion.2 = bf16[384,2048]{1,0:T(8,128)(2,1)S(1)} fusion(f32[384,2048]{1,0:T(8,128)S(1)} %fusion.24, bf16[1024,2048]{1,0:T(8,128)(2,1)} %maximum_dynamic-update-slice_fusion, f32[1024]{0:T(1024)S(1)} %convolution_bitcast_fusion.1, f32[1024,384]{0,1:T(8,128)S(1)} %copy-done.8, f32[1024,384]{0,1:T(8,128)S(1)} %copy-done.10), kind=kOutput, calls=%fused_computation.2 | convolution fusion | flops 1614938112 | bytes 12062720 | tf_op jit(solution)/shard_map/dot_general | solution.py:251
  174.6 4.7 %add_convert_fusion = bf16[1024,2048]{1,0:T(8,128)(2,1)S(1)} fusion(bf16[1024,2048]{1,0:T(8,128)(2,1)} %collective-permute-done.18, f32[1024,2048]{1,0:T(8,128)S(1)} %fusion.4, bf16[1024,384]{0,1:T(8,128)(2,1)S(1)} %get-tuple-element.17, bf16[1,2048,384]{2,1,0:T(8,128)(2,1)S(1)} %copy-done.2), kind=kOutput, calls=%fused_computation | convolution fusion | flops 1619001344 | bytes 19136512 | tf_op jit(solution)/shard_map/dot_general | solution.py:240
  180.0 1.5 collective-permute-start.23
  181.5 4.6 %add_convert_fusion.3 = bf16[2048,384]{1,0:T(8,128)(2,1)S(1)} fusion(f32[2048,384]{1,0:T(8,128)S(1)} %copy-done.19, bf16[1024,2048]{1,0:T(8,128)(2,1)} %maximum_dynamic-update-slice_fusion.1, bf16[1024,384]{0,1:T(8,128)(2,1)S(1)} %get-tuple-element.17), kind=kOutput, calls=%fused_computation.3 | convolution fusion | flops 1612185600 | bytes 9699328 | tf_op jit(solution)/shard_map/dot_general | solution.py:251
  186.2 1.6 collective-permute-start.28
  189.3 4.7 %fusion.49 = f32[2048,384]{1,0:T(8,128)S(1)} fusion(bf16[1024,2048]{1,0:T(8,128)(2,1)} %collective-permute-done.17, bf16[1024,384]{0,1:T(8,128)(2,1)S(1)} %copy-done.6), kind=kOutput, calls=%fused_computation.107 | convolution fusion | flops 1610612736 | bytes 8126464 | tf_op jit(solution)/shard_map/dot_general | solution.py:251
  195.5 6.6 %collective-permute-done.20 = bf16[128,2048]{1,0:T(8,128)(2,1)S(1)} collective-permute-done((bf16[128,2048]{1,0:T(8,128)(2,1)S(1)}, bf16[128,2048]{1,0:T(8,128)(2,1)S(1)}, u32[]{:S(2)}, u32[]{:S(2)}) %collective-permute-start.20) | collective-permute-done | bytes 524320 | tf_op jit(solution)/shard_map/ppermute | solution.py:213
  203.0 4.7 %add_convert_fusion.4 = bf16[2048,384]{1,0:T(8,128)(2,1)S(1)} fusion(f32[2048,384]{1,0:T(8,128)S(1)} %fusion.49, bf16[1024,2048]{1,0:T(8,128)(2,1)} %maximum_dynamic-update-slice_fusion.1, bf16[1024,384]{0,1:T(8,128)(2,1)S(1)} %get-tuple-element.18), kind=kOutput, calls=%fused_computation.4 | convolution fusion | flops 1612185600 | bytes 9699328 | tf_op jit(solution)/shard_map/dot_general | solution.py:251
  207.7 7.2 %collective-permute-done.21 = bf16[128,2048]{1,0:T(8,128)(2,1)S(1)} collective-permute-done((bf16[128,2048]{1,0:T(8,128)(2,1)S(1)}, bf16[128,2048]{1,0:T(8,128)(2,1)S(1)}, u32[]{:S(2)}, u32[]{:S(2)}) %collective-permute-start.21) | collective-permute-done | bytes 524320 | tf_op jit(solution)/shard_map/ppermute | solution.py:213
  216.7 1.6 collective-permute-start.27
  220.8 6.5 %collective-permute-done.25 = bf16[128,2048]{1,0:T(8,128)(2,1)S(1)} collective-permute-done((bf16[128,2048]{1,0:T(8,128)(2,1)S(1)}, bf16[128,2048]{1,0:T(8,128)(2,1)S(1)}, u32[]{:S(2)}, u32[]{:S(2)}) %collective-permute-start.25) | collective-permute-done | bytes 524320 | tf_op jit(solution)/shard_map/ppermute | solution.py:214
  228.8 8.5 %collective-permute-done.27 = bf16[1024,384]{1,0:T(8,128)(2,1)S(1)} collective-permute-done((bf16[1024,384]{1,0:T(8,128)(2,1)S(1)}, bf16[1024,384]{1,0:T(8,128)(2,1)S(1)}, u32[]{:S(2)}, u32[]{:S(2)}) %collective-permute-start.27) | collective-permute-done | bytes 786464 | tf_op jit(solution)/shard_map/ppermute | solution.py:137
  238.4 12.0 %collective-permute-done.29 = bf16[192,2048]{1,0:T(8,128)(2,1)S(1)} collective-permute-done((bf16[192,2048]{1,0:T(8,128)(2,1)S(1)}, bf16[192,2048]{1,0:T(8,128)(2,1)S(1)}, u32[]{:S(2)}, u32[]{:S(2)}) %collective-permute-start.29) | collective-permute-done | bytes 786464 | tf_op jit(solution)/shard_map/ppermute | solution.py:137
  (118 shorter events, 29.3 us)
Async XLA Ops:
  0.6 96.7 %copy-start = (bf16[1,2048,384]{2,1,0:T(8,128)(2,1)S(1)}, bf16[1,2048,384]{2,1,0:T(8,128)(2,1)}, u32[]{:S(2)}) copy-start(bf16[1,2048,384]{2,1,0:T(8,128)(2,1)} %param.12) | copy-start | bytes 4718596
  0.6 16.0 %collective-permute-start.8 = (bf16[128,2048]{1,0:T(8,128)(2,1)}, bf16[128,2048]{1,0:T(8,128)(2,1)S(1)}, u32[]{:S(2)}, u32[]{:S(2)}) collective-permute-start(bf16[128,2048]{1,0:T(8,128)(2,1)} %param.8), channel_id=1, source_target_pairs={{0,4},{1,5},{4,8},{5,9},{8,12},{9,13},{12,14},{13,15},{14,10},{15,... | collective-permute-start | bytes 1572872 | tf_op jit(solution)/shard_map/ppermute | solution.py:181
  3.7 15.1 %collective-permute-start.9 = (bf16[128,2048]{1,0:T(8,128)(2,1)}, bf16[128,2048]{1,0:T(8,128)(2,1)S(1)}, u32[]{:S(2)}, u32[]{:S(2)}) collective-permute-start(bf16[128,2048]{1,0:T(8,128)(2,1)} %param.8), channel_id=1, source_target_pairs={{0,2},{1,3},{4,0},{5,1},{8,4},{9,5},{12,8},{13,9},{14,12},{15,13},... | collective-permute-start | bytes 1572872 | tf_op jit(solution)/shard_map/ppermute | solution.py:182
  3.7 24.1 %collective-permute-start = (bf16[128,2048]{1,0:T(8,128)(2,1)}, bf16[128,2048]{1,0:T(8,128)(2,1)S(1)}, u32[]{:S(2)}, u32[]{:S(2)}) collective-permute-start(bf16[128,2048]{1,0:T(8,128)(2,1)} %param.9), channel_id=1, source_target_pairs={{0,4},{1,5},{4,8},{5,9},{8,12},{9,13},{12,14},{13,15},{14,10},{15,... | collective-permute-start | bytes 1572872 | tf_op jit(solution)/shard_map/ppermute | solution.py:181
  5.8 24.3 %collective-permute-start.1 = (bf16[128,2048]{1,0:T(8,128)(2,1)}, bf16[128,2048]{1,0:T(8,128)(2,1)S(1)}, u32[]{:S(2)}, u32[]{:S(2)}) collective-permute-start(bf16[128,2048]{1,0:T(8,128)(2,1)} %param.9), channel_id=1, source_target_pairs={{0,2},{1,3},{4,0},{5,1},{8,4},{9,5},{12,8},{13,9},{14,12},{15,13},... | collective-permute-start | bytes 1572872 | tf_op jit(solution)/shard_map/ppermute | solution.py:182
  16.6 22.5 %collective-permute-start.10 = (bf16[128,2048]{1,0:T(8,128)(2,1)S(1)}, bf16[128,2048]{1,0:T(8,128)(2,1)S(1)}, u32[]{:S(2)}, u32[]{:S(2)}) collective-permute-start(bf16[128,2048]{1,0:T(8,128)(2,1)S(1)} %collective-permute-done.8), channel_id=1, source_target_pairs={{0,4},{1,5},{4,8},{5,9},{8,12},{9,13},{12,14},{13,15},{14,10},{15,... | collective-permute-start | bytes 1572872 | tf_op jit(solution)/shard_map/ppermute | solution.py:181
  18.8 22.5 %collective-permute-start.11 = (bf16[128,2048]{1,0:T(8,128)(2,1)S(1)}, bf16[128,2048]{1,0:T(8,128)(2,1)S(1)}, u32[]{:S(2)}, u32[]{:S(2)}) collective-permute-start(bf16[128,2048]{1,0:T(8,128)(2,1)S(1)} %collective-permute-done.9), channel_id=1, source_target_pairs={{0,2},{1,3},{4,0},{5,1},{8,4},{9,5},{12,8},{13,9},{14,12},{15,13},... | collective-permute-start | bytes 1572872 | tf_op jit(solution)/shard_map/ppermute | solution.py:182
  27.8 22.5 %collective-permute-start.2 = (bf16[128,2048]{1,0:T(8,128)(2,1)S(1)}, bf16[128,2048]{1,0:T(8,128)(2,1)S(1)}, u32[]{:S(2)}, u32[]{:S(2)}) collective-permute-start(bf16[128,2048]{1,0:T(8,128)(2,1)S(1)} %collective-permute-done), channel_id=1, source_target_pairs={{0,4},{1,5},{4,8},{5,9},{8,12},{9,13},{12,14},{13,15},{14,10},{15,... | collective-permute-start | bytes 1572872 | tf_op jit(solution)/shard_map/ppermute | solution.py:181
  30.0 22.5 %collective-permute-start.3 = (bf16[128,2048]{1,0:T(8,128)(2,1)S(1)}, bf16[128,2048]{1,0:T(8,128)(2,1)S(1)}, u32[]{:S(2)}, u32[]{:S(2)}) collective-permute-start(bf16[128,2048]{1,0:T(8,128)(2,1)S(1)} %collective-permute-done.1), channel_id=1, source_target_pairs={{0,2},{1,3},{4,0},{5,1},{8,4},{9,5},{12,8},{13,9},{14,12},{15,13},... | collective-permute-start | bytes 1572872 | tf_op jit(solution)/shard_map/ppermute | solution.py:182
  39.1 22.5 %collective-permute-start.12 = (bf16[128,2048]{1,0:T(8,128)(2,1)S(1)}, bf16[128,2048]{1,0:T(8,128)(2,1)S(1)}, u32[]{:S(2)}, u32[]{:S(2)}) collective-permute-start(bf16[128,2048]{1,0:T(8,128)(2,1)S(1)} %collective-permute-done.10), channel_id=1, source_target_pairs={{0,4},{1,5},{4,8},{5,9},{8,12},{9,13},{12,14},{13,15},{14,10},{15,... | collective-permute-start | bytes 1572872 | tf_op jit(solution)/shard_map/ppermute | solution.py:181
  41.3 22.5 %collective-permute-start.13 = (bf16[128,2048]{1,0:T(8,128)(2,1)S(1)}, bf16[128,2048]{1,0:T(8,128)(2,1)S(1)}, u32[]{:S(2)}, u32[]{:S(2)}) collective-permute-start(bf16[128,2048]{1,0:T(8,128)(2,1)S(1)} %collective-permute-done.11), channel_id=1, source_target_pairs={{0,2},{1,3},{4,0},{5,1},{8,4},{9,5},{12,8},{13,9},{14,12},{15,13},... | collective-permute-start | bytes 1572872 | tf_op jit(solution)/shard_map/ppermute | solution.py:182
  50.3 31.4 %collective-permute-start.4 = (bf16[128,2048]{1,0:T(8,128)(2,1)S(1)}, bf16[128,2048]{1,0:T(8,128)(2,1)S(1)}, u32[]{:S(2)}, u32[]{:S(2)}) collective-permute-start(bf16[128,2048]{1,0:T(8,128)(2,1)S(1)} %collective-permute-done.2), channel_id=1, source_target_pairs={{0,4},{1,5},{4,8},{5,9},{8,12},{9,13},{12,14},{13,15},{14,10},{15,... | collective-permute-start | bytes 1572872 | tf_op jit(solution)/shard_map/ppermute | solution.py:181
  52.5 30.9 %collective-permute-start.5 = (bf16[128,2048]{1,0:T(8,128)(2,1)S(1)}, bf16[128,2048]{1,0:T(8,128)(2,1)S(1)}, u32[]{:S(2)}, u32[]{:S(2)}) collective-permute-start(bf16[128,2048]{1,0:T(8,128)(2,1)S(1)} %collective-permute-done.3), channel_id=1, source_target_pairs={{0,2},{1,3},{4,0},{5,1},{8,4},{9,5},{12,8},{13,9},{14,12},{15,13},... | collective-permute-start | bytes 1572872 | tf_op jit(solution)/shard_map/ppermute | solution.py:182
  61.6 16.0 %collective-permute-start.14 = (bf16[128,1024]{1,0:T(8,128)(2,1)S(1)}, bf16[128,1024]{1,0:T(8,128)(2,1)S(1)}, u32[]{:S(2)}, u32[]{:S(2)}) collective-permute-start(bf16[128,1024]{1,0:T(8,128)(2,1)S(1)} %slice.72), channel_id=1, source_target_pairs={{0,4},{1,5},{4,8},{5,9},{8,12},{9,13},{12,14},{13,15},{14,10},{15,... | collective-permute-start | bytes 786440 | tf_op jit(solution)/shard_map/ppermute | solution.py:187
  63.8 15.3 %collective-permute-start.15 = (bf16[128,1024]{1,0:T(8,128)(2,1)S(1)}, bf16[128,1024]{1,0:T(8,128)(2,1)S(1)}, u32[]{:S(2)}, u32[]{:S(2)}) collective-permute-start(bf16[128,1024]{1,0:T(8,128)(2,1)S(1)} %slice.73), channel_id=1, source_target_pairs={{0,2},{1,3},{4,0},{5,1},{8,4},{9,5},{12,8},{13,9},{14,12},{15,13},... | collective-permute-start | bytes 786440 | tf_op jit(solution)/shard_map/ppermute | solution.py:188
  80.0 28.1 %collective-permute-start.17 = (bf16[1024,2048]{1,0:T(8,128)(2,1)}, bf16[1024,2048]{1,0:T(8,128)(2,1)}, u32[]{:S(2)}, u32[]{:S(2)}) collective-permute-start(bf16[1024,2048]{1,0:T(8,128)(2,1)} %maximum_dynamic-update-slice_fusion.1), channel_id=1, source_target_pairs={{0,1},{1,0},{2,3},{3,2},{4,5},{5,4},{6,7},{7,6},{8,9},{9,8},{10,11... | collective-permute-start | bytes 12582920 | tf_op jit(solution)/shard_map/ppermute | solution.py:194
  81.7 8.8 %collective-permute-start.6 = (bf16[128,1024]{1,0:T(8,128)(2,1)S(1)}, bf16[128,1024]{1,0:T(8,128)(2,1)S(1)}, u32[]{:S(2)}, u32[]{:S(2)}) collective-permute-start(bf16[128,1024]{1,0:T(8,128)(2,1)S(1)} %slice.70), channel_id=1, source_target_pairs={{0,4},{1,5},{4,8},{5,9},{8,12},{9,13},{12,14},{13,15},{14,10},{15,... | collective-permute-start | bytes 786440 | tf_op jit(solution)/shard_map/ppermute | solution.py:187
  83.4 9.9 %copy-start.17 = (s32[8]{0:T(128)S(1)}, s32[8]{0:T(128)}, u32[]{:S(2)}) copy-start(s32[8]{0:T(128)} %constant.79.clone) | copy-start | bytes 100
  83.4 9.9 %copy-start.2 = (bf16[1,2048,384]{2,1,0:T(8,128)(2,1)S(1)}, bf16[1,2048,384]{2,1,0:T(8,128)(2,1)}, u32[]{:S(2)}) copy-start(bf16[1,2048,384]{2,1,0:T(8,128)(2,1)} %param.13) | copy-start | bytes 4718596
  83.4 9.0 %collective-permute-start.7 = (bf16[128,1024]{1,0:T(8,128)(2,1)S(1)}, bf16[128,1024]{1,0:T(8,128)(2,1)S(1)}, u32[]{:S(2)}, u32[]{:S(2)}) collective-permute-start(bf16[128,1024]{1,0:T(8,128)(2,1)S(1)} %slice.71), channel_id=1, source_target_pairs={{0,2},{1,3},{4,0},{5,1},{8,4},{9,5},{12,8},{13,9},{14,12},{15,13},... | collective-permute-start | bytes 786440 | tf_op jit(solution)/shard_map/ppermute | solution.py:188
  93.3 23.5 %collective-permute-start.16 = (bf16[1024,2048]{1,0:T(8,128)(2,1)}, bf16[1024,2048]{1,0:T(8,128)(2,1)}, u32[]{:S(2)}, u32[]{:S(2)}) collective-permute-start(bf16[1024,2048]{1,0:T(8,128)(2,1)} %maximum_dynamic-update-slice_fusion), channel_id=1, source_target_pairs={{0,1},{1,0},{2,3},{3,2},{4,5},{5,4},{6,7},{7,6},{8,9},{9,8},{10,11... | collective-permute-start | bytes 12582920 | tf_op jit(solution)/shard_map/ppermute | solution.py:194
  97.3 4.6 %copy-start.7 = (f32[1024,384]{0,1:T(8,128)}, f32[1024,384]{0,1:T(8,128)S(1)}, u32[]{:S(2)}) copy-start(f32[1024,384]{0,1:T(8,128)S(1)} %fusion.12) | copy-start | bytes 4718596
  97.4 4.6 %copy-start.18 = (bf16[1,384,2048]{2,1,0:T(8,128)(2,1)S(1)}, bf16[1,384,2048]{2,1,0:T(8,128)(2,1)}, u32[]{:S(2)}) copy-start(bf16[1,384,2048]{2,1,0:T(8,128)(2,1)} %param.14) | copy-start | bytes 4718596
  102.0 5.8 %copy-start.9 = (f32[1024,384]{0,1:T(8,128)}, f32[1024,384]{0,1:T(8,128)S(1)}, u32[]{:S(2)}) copy-start(f32[1024,384]{0,1:T(8,128)S(1)} %fusion.6) | copy-start | bytes 4718596
  112.1 4.6 %copy-start.11 = (f32[1024,384]{0,1:T(8,128)}, f32[1024,384]{0,1:T(8,128)S(1)}, u32[]{:S(2)}) copy-start(f32[1024,384]{0,1:T(8,128)S(1)} %fusion.2) | copy-start | bytes 4718596
  116.7 5.8 %copy-start.13 = (f32[1024,384]{0,1:T(8,128)}, f32[1024,384]{0,1:T(8,128)S(1)}, u32[]{:S(2)}) copy-start(f32[1024,384]{0,1:T(8,128)S(1)} %fusion.9) | copy-start | bytes 4718596
  116.7 10.7 %copy-start.16 = (bf16[128,4]{0,1:T(4,128)(2,1)S(1)}, bf16[128,4]{0,1:T(4,128)(2,1)}, u32[]{:S(2)}) copy-start(bf16[128,4]{0,1:T(4,128)(2,1)} %param.11) | copy-start | bytes 3076
  116.7 17.0 %copy-start.15 = (s32[128,4]{0,1:T(4,128)S(1)}, s32[128,4]{0,1:T(4,128)}, u32[]{:S(2)}) copy-start(s32[128,4]{0,1:T(4,128)} %param.10) | copy-start | bytes 6148
  123.4 10.3 %all-to-all-start.1 = ((bf16[16,1,128]{2,1,0:T(2,128)(2,1)}), bf16[16,1,128]{2,1,0:T(2,128)(2,1)S(1)}, u32[]{:S(2)}, u32[]{:S(2)}) async-start(bf16[16,1,128]{2,1,0:T(2,128)(2,1)} %copy.26), calls=%async_computation.1 | async-start | bytes 16384 | tf_op jit(solution)/shard_map/all_to_all | solution.py:263
  146.8 2.4 copy-start.5
  153.8 20.8 %collective-permute-start.18 = (bf16[1024,2048]{1,0:T(8,128)(2,1)}, bf16[1024,2048]{1,0:T(8,128)(2,1)}, u32[]{:S(2)}, u32[]{:S(2)}) collective-permute-start(bf16[1024,2048]{1,0:T(8,128)(2,1)} %add_convert_fusion.1), channel_id=1, source_target_pairs={{0,1},{1,0},{2,3},{3,2},{4,5},{5,4},{6,7},{7,6},{8,9},{9,8},{10,11... | collective-permute-start | bytes 12582920 | tf_op jit(solution)/shard_map/ppermute | solution.py:244
  159.7 6.4 %copy-start.12 = (f32[1024,384]{0,1:T(8,128)S(1)}, f32[1024,384]{0,1:T(8,128)}, u32[]{:S(2)}) copy-start(f32[1024,384]{0,1:T(8,128)} %copy-done.11) | copy-start | bytes 4718596
  159.7 6.4 %copy-start.14 = (f32[1024,384]{0,1:T(8,128)S(1)}, f32[1024,384]{0,1:T(8,128)}, u32[]{:S(2)}) copy-start(f32[1024,384]{0,1:T(8,128)} %copy-done.13) | copy-start | bytes 4718596
  166.1 4.4 %copy-start.8 = (f32[1024,384]{0,1:T(8,128)S(1)}, f32[1024,384]{0,1:T(8,128)}, u32[]{:S(2)}) copy-start(f32[1024,384]{0,1:T(8,128)} %copy-done.7) | copy-start | bytes 4718596
  166.1 4.4 %copy-start.10 = (f32[1024,384]{0,1:T(8,128)S(1)}, f32[1024,384]{0,1:T(8,128)}, u32[]{:S(2)}) copy-start(f32[1024,384]{0,1:T(8,128)} %copy-done.9) | copy-start | bytes 4718596
  174.6 6.9 %copy-start.19 = (f32[2048,384]{1,0:T(8,128)S(1)}, f32[2048,384]{1,0:T(8,128)}, u32[]{:S(2)}) copy-start(f32[2048,384]{1,0:T(8,128)} %fusion.50) | copy-start | bytes 9437188
  179.4 8.8 %collective-permute-start.19 = (bf16[128,1024]{1,0:T(8,128)(2,1)S(1)}, bf16[128,1024]{1,0:T(8,128)(2,1)S(1)}, u32[]{:S(2)}, u32[]{:S(2)}) collective-permute-start(bf16[128,1024]{1,0:T(8,128)(2,1)S(1)} %get-tuple-element.13), channel_id=1, source_target_pairs={{0,4},{1,5},{4,8},{5,9},{8,12},{9,13},{12,14},{13,15},{14,10},{15,... | collective-permute-start | bytes 786440 | tf_op jit(solution)/shard_map/ppermute | solution.py:204
  180.0 8.4 %collective-permute-start.23 = (bf16[128,1024]{1,0:T(8,128)(2,1)S(1)}, bf16[128,1024]{1,0:T(8,128)(2,1)S(1)}, u32[]{:S(2)}, u32[]{:S(2)}) collective-permute-start(bf16[128,1024]{1,0:T(8,128)(2,1)S(1)} %get-tuple-element.14), channel_id=1, source_target_pairs={{0,2},{1,3},{4,0},{5,1},{8,4},{9,5},{12,8},{13,9},{14,12},{15,13},... | collective-permute-start | bytes 786440 | tf_op jit(solution)/shard_map/ppermute | solution.py:205
  186.2 3.1 %copy-start.6 = (bf16[1024,384]{0,1:T(8,128)(2,1)S(1)}, bf16[1024,384]{0,1:T(8,128)(2,1)}, u32[]{:S(2)}) copy-start(bf16[1024,384]{0,1:T(8,128)(2,1)} %copy-done.5) | copy-start | bytes 2359300
  186.2 32.8 %collective-permute-start.28 = (bf16[1024,384]{1,0:T(8,128)(2,1)S(1)}, bf16[1024,384]{1,0:T(8,128)(2,1)S(1)}, u32[]{:S(2)}, u32[]{:S(2)}) collective-permute-start(bf16[1024,384]{1,0:T(8,128)(2,1)S(1)} %constant_dynamic-slice_fusion.1), channel_id=1, source_target_pairs={{0,16},{16,0},{1,17},{17,1},{2,18},{18,2},{3,19},{19,3},{4,20},{20... | collective-permute-start | bytes 2359304 | tf_op jit(solution)/shard_map/ppermute | solution.py:137
  188.6 13.4 %collective-permute-start.20 = (bf16[128,2048]{1,0:T(8,128)(2,1)S(1)}, bf16[128,2048]{1,0:T(8,128)(2,1)S(1)}, u32[]{:S(2)}, u32[]{:S(2)}) collective-permute-start(bf16[128,2048]{1,0:T(8,128)(2,1)S(1)} %pad_maximum_fusion), channel_id=1, source_target_pairs={{0,4},{1,5},{4,8},{5,9},{8,12},{9,13},{12,14},{13,15},{14,10},{15,... | collective-permute-start | bytes 1572872 | tf_op jit(solution)/shard_map/ppermute | solution.py:213
  194.0 13.7 %collective-permute-start.24 = (bf16[128,2048]{1,0:T(8,128)(2,1)S(1)}, bf16[128,2048]{1,0:T(8,128)(2,1)S(1)}, u32[]{:S(2)}, u32[]{:S(2)}) collective-permute-start(bf16[128,2048]{1,0:T(8,128)(2,1)S(1)} %pad_maximum_fusion.1), channel_id=1, source_target_pairs={{0,2},{1,3},{4,0},{5,1},{8,4},{9,5},{12,8},{13,9},{14,12},{15,13},... | collective-permute-start | bytes 1572872 | tf_op jit(solution)/shard_map/ppermute | solution.py:214
  202.2 12.7 %collective-permute-start.21 = (bf16[128,2048]{1,0:T(8,128)(2,1)S(1)}, bf16[128,2048]{1,0:T(8,128)(2,1)S(1)}, u32[]{:S(2)}, u32[]{:S(2)}) collective-permute-start(bf16[128,2048]{1,0:T(8,128)(2,1)S(1)} %add_convert_fusion.12), channel_id=1, source_target_pairs={{0,4},{1,5},{4,8},{5,9},{8,12},{9,13},{12,14},{13,15},{14,10},{15,... | collective-permute-start | bytes 1572872 | tf_op jit(solution)/shard_map/ppermute | solution.py:213
  215.3 12.0 %collective-permute-start.25 = (bf16[128,2048]{1,0:T(8,128)(2,1)S(1)}, bf16[128,2048]{1,0:T(8,128)(2,1)S(1)}, u32[]{:S(2)}, u32[]{:S(2)}) collective-permute-start(bf16[128,2048]{1,0:T(8,128)(2,1)S(1)} %get-tuple-element.10), channel_id=1, source_target_pairs={{0,2},{1,3},{4,0},{5,1},{8,4},{9,5},{12,8},{13,9},{14,12},{15,13},... | collective-permute-start | bytes 1572872 | tf_op jit(solution)/shard_map/ppermute | solution.py:214
  216.7 20.5 %collective-permute-start.27 = (bf16[1024,384]{1,0:T(8,128)(2,1)S(1)}, bf16[1024,384]{1,0:T(8,128)(2,1)S(1)}, u32[]{:S(2)}, u32[]{:S(2)}) collective-permute-start(bf16[1024,384]{1,0:T(8,128)(2,1)S(1)} %constant_dynamic-slice_fusion.2), channel_id=1, source_target_pairs={{0,16},{16,0},{1,17},{17,1},{2,18},{18,2},{3,19},{19,3},{4,20},{20... | collective-permute-start | bytes 2359304 | tf_op jit(solution)/shard_map/ppermute | solution.py:137
  218.4 32.0 %collective-permute-start.29 = (bf16[192,2048]{1,0:T(8,128)(2,1)S(1)}, bf16[192,2048]{1,0:T(8,128)(2,1)S(1)}, u32[]{:S(2)}, u32[]{:S(2)}) collective-permute-start(bf16[192,2048]{1,0:T(8,128)(2,1)S(1)} %constant_dynamic-slice_fusion), channel_id=1, source_target_pairs={{0,16},{16,0},{1,17},{17,1},{2,18},{18,2},{3,19},{19,3},{4,20},{20... | collective-permute-start | bytes 2359304 | tf_op jit(solution)/shard_map/ppermute | solution.py:137
  220.1 31.5 %collective-permute-start.22 = (bf16[128,2048]{1,0:T(8,128)(2,1)S(1)}, bf16[128,2048]{1,0:T(8,128)(2,1)S(1)}, u32[]{:S(2)}, u32[]{:S(2)}) collective-permute-start(bf16[128,2048]{1,0:T(8,128)(2,1)S(1)} %get-tuple-element.9), channel_id=1, source_target_pairs={{0,4},{1,5},{4,8},{5,9},{8,12},{9,13},{12,14},{13,15},{14,10},{15,... | collective-permute-start | bytes 1572872 | tf_op jit(solution)/shard_map/ppermute | solution.py:213
  227.4 24.2 %collective-permute-start.26 = (bf16[128,2048]{1,0:T(8,128)(2,1)S(1)}, bf16[128,2048]{1,0:T(8,128)(2,1)S(1)}, u32[]{:S(2)}, u32[]{:S(2)}) collective-permute-start(bf16[128,2048]{1,0:T(8,128)(2,1)S(1)} %add_convert_fusion.9), channel_id=1, source_target_pairs={{0,2},{1,3},{4,0},{5,1},{8,4},{9,5},{12,8},{13,9},{14,12},{15,13},... | collective-permute-start | bytes 1572872 | tf_op jit(solution)/shard_map/ppermute | solution.py:214
  (3 other events, 7.0 us)

commit v4 on v3

--- a/solution.py
+++ b/solution.py
@@ -174,12 +174,14 @@
         dense.astype(BF16).T, "exp", split_axis=0, concat_axis=0, tiled=True
     ).reshape(members, local)
 
-    def gather(rows):
+    def gather(rows, beside):
         blocks = [rows]
         right = left = rows
-        for _ in range(1, half):
+        for step in range(1, half):
             right = lax.ppermute(right, "exp", ahead)
             left = lax.ppermute(left, "exp", behind)
+            if step == 1:
+                right, beside = lax.optimization_barrier((right, beside))
             blocks += [right, left]
         blocks.append(
             jnp.concatenate(
@@ -191,7 +193,7 @@
             )
         )
         own = jnp.concatenate(blocks, axis=0)
-        return own, lax.ppermute(own, "exp", swap)
+        return (own, lax.ppermute(own, "exp", swap)), beside
 
     def give_back(terms):
         def term(offset):
@@ -215,8 +217,8 @@
         total = term(0).astype(F32) + right.astype(F32) + left.astype(F32)
         return total.astype(BF16)
 
-    rows = gather(tokens)
-    grads = gather(out_grad)
+    rows, weight = gather(tokens, weight)
+    grads, weight = gather(out_grad, weight)
     wg, wu, wd = w_gate[0], w_up[0], w_down[0]
     over_last = (((1,), (1,)), ((), ()))
     over_rows = (((0,), (0,)), ((), ()))
@@ -251,15 +253,18 @@
             lax.dot_general(a, b, over_rows, preferred_element_type=F32)
             for a, b in zip(left, right)
         )
-        return across(total.astype(BF16), "rep")[None]
+        return total.astype(BF16)
 
     scaled, d_gate, d_up = ((near[n], far[n]) for n in (1, 2, 3))
-    grad_gate = outer(rows, d_gate)
-    grad_up = outer(rows, d_up)
-    grad_down = outer(scaled, grads)
+    gate_total = outer(rows, d_gate)
+    up_total = outer(rows, d_up)
+    down_total = outer(scaled, grads)
+    grad_gate = across(gate_total, "rep")[None]
+    grad_up = across(up_total, "rep")[None]
     term = lax.dot_general(near_pick, near[0], over_rows, preferred_element_type=F32)
     term += lax.dot_general(far_pick, far[0], over_rows, preferred_element_type=F32)
-    term = term.astype(BF16)
+    term, down_total = lax.optimization_barrier((term.astype(BF16), down_total))
+    grad_down = across(down_total, "rep")[None]
     term = lax.all_to_all(term, "exp", split_axis=0, concat_axis=0, tiled=True)
     picked = jnp.where(hit, term.astype(F32).T[:, None, :], 0.0)
     grad_prob = jnp.sum(picked, axis=2).astype(BF16)

time: 256 us -> 218 us (0.85)
  waiting for transfers between devices: 106 us -> 82.2 us
  matrix products: 72.4 us -> 56.1 us
  blocking collectives: 8.97 us -> 0 us
  local copies, waits for them, and re-layouts: 15.1 us -> 20.4 us
  starting transfers between devices: 34.8 us -> 39 us
    ppermute x6, waiting for transfers between devices: 38.1 us -> 23.3 us  [gather(): right = lax.ppermute(right, 'exp', ahead)]
    all_to_all x0 -> x1, waiting for transfers between devices: none -> 12.7 us  [gathered_body(): lax.all_to_all(dense.astype(BF16).T, 'exp', split_axis=0, concat_axis=0,...]
    ppermute x3, waiting for transfers between devices: 20.5 us -> 9.53 us  [across(): arrived = lax.ppermute(theirs, axis, [(0, 1), (1, 0)])]
    all_to_all x1 -> x0, blocking collectives: 8.97 us -> none  [gathered_body(): lax.all_to_all(dense.astype(BF16).T, 'exp', split_axis=0, concat_axis=0,...]
    convert_element_type x2 -> x0, other arithmetic: 6.62 us -> none  [forward(): d_up = (d_back * active).astype(BF16)]
    ppermute x3, waiting for transfers between devices: 6.47 us -> 0.01 us  [give_back(): left = lax.ppermute(left, 'exp', behind)]
    all_to_all x0 -> x1, starting transfers between devices: none -> 6.36 us  [gathered_body(): lax.all_to_all(dense.astype(BF16).T, 'exp', split_axis=0, concat_axis=0,...]
    ppermute x6, starting transfers between devices: 13.7 us -> 7.4 us  [gather(): right = lax.ppermute(right, 'exp', ahead)]
  transfers between devices with their start and end apart: 31 -> 32, of which waited for: 17 -> 14; matrix products, arithmetic and copies ran while one was open for 31% -> 37% of each run, Pallas kernels for 0% -> 0%
where the time goes in v4:
time: 218 us; the launch traced here: 215 us
  waiting for transfers between devices  82.2 us (38%)
  matrix products  56.1 us (26%)
  starting transfers between devices  39 us (18%)
  local copies, waits for them, and re-layouts  20.4 us (9%)
  other arithmetic  15.8 us (7%)
    dot_general x6, matrix products, outer(): lax.dot_general(a, b, over_rows, preferred_element_type=F32)  23.4 us
    ppermute x6, waiting for transfers between devices, gather(): right = lax.ppermute(right, 'exp', ahead)  23.3 us
    ppermute x2, waiting for transfers between devices, gather(): lax.ppermute(right[:, :middle], 'exp', ahead)  16.6 us
    unnamed x41, local copies, waits for them, and re-layouts  15 us
    ppermute x3, waiting for transfers between devices, give_back(): right = lax.ppermute(right, 'exp', ahead)  12.9 us
    all_to_all x1, waiting for transfers between devices, gathered_body(): lax.all_to_all(dense.astype(BF16).T, 'exp', split_axis=0, concat_axis=0,...  12.7 us
    dot_general x2, matrix products, forward(): lax.dot_general(grads[side], wd, over_last, preferred_element_type=F32)  9.77 us
    ppermute x3, waiting for transfers between devices, across(): arrived = lax.ppermute(theirs, axis, [(0, 1), (1, 0)])  9.53 us
  transfers between devices with their start and end apart: 32, of which 14 were waited for; matrix products, arithmetic and copies ran while one was open for 37% of the time, Pallas kernels for 0%

profile of v4, /device:TPU:0, one launch (start us, length us, event | category | flops | bytes accessed | tf_op | source)
XLA Modules:
  0.0 214.7 jit_solution(6655713855567487628)
XLA Ops:
  0.6 3.1 %collective-permute-start.1 = (bf16[128,2048]{1,0:T(8,128)(2,1)}, bf16[128,2048]{1,0:T(8,128)(2,1)}, u32[]{:S(2)}, u32[]{:S(2)}) collective-permute-start(bf16[128,2048]{1,0:T(8,128)(2,1)} %param.8), channel_id=1, source_target_pairs={{0,4},{1,5},{4,8},{5,9},{8,12},{9,13},{12,14},{13,15},{14,10},{15,... | collective-permute-start | bytes 1572872 | tf_op jit(solution)/shard_map/ppermute | solution.py:181
  3.7 2.0 collective-permute-start
  7.7 6.4 %all-to-all-start = ((bf16[16,1,128]{2,1,0:T(2,128)(2,1)}), bf16[16,1,128]{2,1,0:T(2,128)(2,1)S(1)}, u32[]{:S(2)}, u32[]{:S(2)}) async-start(bf16[16,1,128]{2,1,0:T(2,128)(2,1)} %copy.25), calls=%async_computation | async-start | bytes 16384 | tf_op jit(solution)/shard_map/all_to_all | solution.py:173
  14.1 1.9 constant_dynamic-update-slice_fusion.13
  16.0 1.9 constant_dynamic-update-slice_fusion.6
  17.9 12.7 %all-to-all-done = bf16[16,1,128]{2,1,0:T(2,128)(2,1)S(1)} async-done(((bf16[16,1,128]{2,1,0:T(2,128)(2,1)}), bf16[16,1,128]{2,1,0:T(2,128)(2,1)S(1)}, u32[]{:S(2)}, u32[]{:S(2)}) %all-to-all-start) | async-done | bytes 4128 | tf_op jit(solution)/shard_map/all_to_all | solution.py:173
  31.2 1.5 collective-permute-start.11
  32.7 1.9 constant_dynamic-update-slice_fusion.12
  35.1 1.5 collective-permute-start.4
  38.3 7.4 %collective-permute-done.10 = bf16[128,2048]{1,0:T(8,128)(2,1)S(1)} collective-permute-done((bf16[128,2048]{1,0:T(8,128)(2,1)}, bf16[128,2048]{1,0:T(8,128)(2,1)S(1)}, u32[]{:S(2)}, u32[]{:S(2)}) %collective-permute-start.10) | collective-permute-done | bytes 524320 | tf_op jit(solution)/shard_map/ppermute | solution.py:181
  46.2 1.5 collective-permute-start.13
  48.5 8.4 %collective-permute-done.3 = bf16[128,2048]{1,0:T(8,128)(2,1)S(1)} collective-permute-done((bf16[128,2048]{1,0:T(8,128)(2,1)S(1)}, bf16[128,2048]{1,0:T(8,128)(2,1)S(1)}, u32[]{:S(2)}, u32[]{:S(2)}) %collective-permute-start.3) | collective-permute-done | bytes 524320 | tf_op jit(solution)/shard_map/ppermute | solution.py:181
  57.5 1.5 collective-permute-start.6
  60.6 7.5 %collective-permute-done.12 = bf16[128,2048]{1,0:T(8,128)(2,1)S(1)} collective-permute-done((bf16[128,2048]{1,0:T(8,128)(2,1)S(1)}, bf16[128,2048]{1,0:T(8,128)(2,1)S(1)}, u32[]{:S(2)}, u32[]{:S(2)}) %collective-permute-start.12) | collective-permute-done | bytes 524320 | tf_op jit(solution)/shard_map/ppermute | solution.py:181
  68.8 1.5 collective-permute-start.15
  72.0 11.9 %collective-permute-done.14 = bf16[128,1024]{1,0:T(8,128)(2,1)S(1)} collective-permute-done((bf16[128,1024]{1,0:T(8,128)(2,1)S(1)}, bf16[128,1024]{1,0:T(8,128)(2,1)S(1)}, u32[]{:S(2)}, u32[]{:S(2)}) %collective-permute-start.14) | collective-permute-done | bytes 262176 | tf_op jit(solution)/shard_map/ppermute | solution.py:189
  87.5 1.4 collective-permute-start.8
  90.6 4.7 %collective-permute-done.7 = bf16[128,1024]{1,0:T(8,128)(2,1)S(1)} collective-permute-done((bf16[128,1024]{1,0:T(8,128)(2,1)S(1)}, bf16[128,1024]{1,0:T(8,128)(2,1)S(1)}, u32[]{:S(2)}, u32[]{:S(2)}) %collective-permute-start.7) | collective-permute-done | bytes 262176 | tf_op jit(solution)/shard_map/ppermute | solution.py:189
  97.4 4.1 %fusion.2 = f32[1024,384]{0,1:T(8,128)S(1)} fusion(bf16[1024,2048]{1,0:T(8,128)(2,1)} %collective-permute-done.17, bf16[1,2048,384]{2,1,0:T(8,128)(2,1)S(1)} %copy-done), kind=kOutput, calls=%fused_computation.7 | convolution fusion | flops 1610612736 | bytes 7340032 | tf_op jit(solution)/shard_map/dot_general | solution.py:229
  101.6 4.1 %fusion.9 = f32[1024,384]{0,1:T(8,128)S(1)} fusion(bf16[1024,2048]{1,0:T(8,128)(2,1)} %collective-permute-done.17, bf16[1,2048,384]{2,1,0:T(8,128)(2,1)S(1)} %copy-done.3), kind=kOutput, calls=%fused_computation.14 | convolution fusion | flops 1610612736 | bytes 7340032 | tf_op jit(solution)/shard_map/dot_general | solution.py:230
  105.8 5.2 %multiply_reduce_fusion = (bf16[1024]{0:T(1024)(128)(2,1)S(1)}, bf16[1024,384]{0,1:T(8,128)(2,1)S(1)}, bf16[1024,384]{0,1:T(8,128)(2,1)S(1)}) fusion(f32[1024,384]{0,1:T(8,128)S(1)} %fusion.9, f32[1024,384]{0,1:T(8,128)S(1)} %fusion.2, f32[1024]{0:T(1024)S(1)} %convolution_bitcast_fusion, bf16[1024,2048]{1,0:T(8,128)(2,1)} %collective-permute-done.16, ...), kind=kOutput, calls=%fused_computation.28 | convolution fusion | flops 1617296384 | bytes 10491904 | tf_op jit(solution)/shard_map/dot_general | solution.py:231
  110.9 2.4 %fusion = f32[1024,2048]{1,0:T(8,128)S(1)} fusion(bf16[1024,384]{0,1:T(8,128)(2,1)S(1)} %get-tuple-element.20, bf16[1,2048,384]{2,1,0:T(8,128)(2,1)S(1)} %copy-done), kind=kOutput, calls=%fused_computation.5 | convolution fusion | flops 1610612736 | bytes 10747904 | tf_op jit(solution)/shard_map/dot_general | solution.py:241
  113.3 2.4 %add_convert_fusion.1 = bf16[1024,2048]{1,0:T(8,128)(2,1)S(1)} fusion(f32[1024,2048]{1,0:T(8,128)S(1)} %fusion, bf16[1024,384]{0,1:T(8,128)(2,1)S(1)} %get-tuple-element.32, bf16[1,2048,384]{2,1,0:T(8,128)(2,1)S(1)} %copy-done.3), kind=kOutput, calls=%fused_computation.1 | convolution fusion | flops 1614807040 | bytes 14942208 | tf_op jit(solution)/shard_map/dot_general | solution.py:242
  116.3 1.9 fusion.12
  118.2 2.3 %fusion.6 = f32[1024,384]{0,1:T(8,128)S(1)} fusion(bf16[1024,2048]{1,0:T(8,128)(2,1)S(1)} %copy-done.6, bf16[1,2048,384]{2,1,0:T(8,128)(2,1)S(1)} %copy-done), kind=kOutput, calls=%fused_computation.11 | convolution fusion | flops 1610612736 | bytes 7340032 | tf_op jit(solution)/shard_map/dot_general | solution.py:229
  120.5 4.6 %multiply_reduce_fusion.1 = (bf16[1024]{0:T(1024)(128)(2,1)S(1)}, bf16[1024,384]{0,1:T(8,128)(2,1)S(1)}, bf16[1024,384]{0,1:T(8,128)(2,1)S(1)}) fusion(f32[1024,384]{0,1:T(8,128)S(1)} %fusion.12, f32[1024,384]{0,1:T(8,128)S(1)} %fusion.6, f32[1024]{0:T(1024)S(1)} %convolution_bitcast_fusion.1, bf16[1024,2048]{1,0:T(8,128)(2,1)} %maximum_dynamic-update-slice_fusion, ...), kind=kOutput, calls=%fused_computation.29 | convolution fusion | flops 1617296384 | bytes 10491904 | tf_op jit(solution)/shard_map/dot_general | solution.py:231
  125.4 2.4 %fusion.4 = f32[1024,2048]{1,0:T(8,128)S(1)} fusion(bf16[1024,384]{0,1:T(8,128)(2,1)S(1)} %get-tuple-element.22, bf16[1,2048,384]{2,1,0:T(8,128)(2,1)S(1)} %copy-done), kind=kOutput, calls=%fused_computation.9 | convolution fusion | flops 1610612736 | bytes 10747904 | tf_op jit(solution)/shard_map/dot_general | solution.py:241
  128.0 4.1 %fusion.21 = f32[384,2048]{1,0:T(8,128)S(1)} fusion(bf16[1024,2048]{1,0:T(8,128)(2,1)} %collective-permute-done.16, f32[1024]{0:T(1024)S(1)} %convolution_bitcast_fusion, f32[1024,384]{0,1:T(8,128)S(1)} %copy-done.12, f32[1024,384]{0,1:T(8,128)S(1)} %fusion.2), kind=kOutput, calls=%fused_computation.47 | convolution fusion | flops 1613365248 | bytes 10489856 | tf_op jit(solution)/shard_map/dot_general | solution.py:253
  132.1 4.0 %add_convert_fusion.4 = bf16[384,2048]{1,0:T(8,128)(2,1)S(1)} fusion(f32[384,2048]{1,0:T(8,128)S(1)} %fusion.21, bf16[1024,2048]{1,0:T(8,128)(2,1)} %maximum_dynamic-update-slice_fusion, f32[1024]{0:T(1024)S(1)} %convolution_bitcast_fusion.1, f32[1024,384]{0,1:T(8,128)S(1)} %fusion.12, f32[1024,384]{0,1:T(8,128)S(1)} %fusion.6), kind=kOutput, calls=%fused_computation.4 | convolution fusion | flops 1614938112 | bytes 12062720 | tf_op jit(solution)/shard_map/dot_general | solution.py:253
  137.1 1.5 collective-permute-start.29
  138.7 2.4 %add_convert_fusion = bf16[1024,2048]{1,0:T(8,128)(2,1)S(1)} fusion(bf16[1024,2048]{1,0:T(8,128)(2,1)S(1)} %collective-permute-done.18, f32[1024,2048]{1,0:T(8,128)S(1)} %fusion.4, bf16[1024,384]{0,1:T(8,128)(2,1)S(1)} %get-tuple-element.31, bf16[1,2048,384]{2,1,0:T(8,128)(2,1)S(1)} %copy-done.3), kind=kOutput, calls=%fused_computation | convolution fusion | flops 1619001344 | bytes 19136512 | tf_op jit(solution)/shard_map/dot_general | solution.py:242
  141.2 1.5 collective-permute-start.19
  143.4 4.7 %fusion.45 = f32[2048,384]{1,0:T(8,128)S(1)} fusion(bf16[1024,2048]{1,0:T(8,128)(2,1)} %collective-permute-done.17, bf16[1024,384]{0,1:T(8,128)(2,1)S(1)} %get-tuple-element.32), kind=kOutput, calls=%fused_computation.104 | convolution fusion | flops 1610612736 | bytes 8126464 | tf_op jit(solution)/shard_map/dot_general | solution.py:253
  151.3 2.4 %add_convert_fusion.2 = bf16[2048,384]{1,0:T(8,128)(2,1)S(1)} fusion(f32[2048,384]{1,0:T(8,128)S(1)} %fusion.45, bf16[1024,2048]{1,0:T(8,128)(2,1)S(1)} %copy-done.7, bf16[1024,384]{0,1:T(8,128)(2,1)S(1)} %get-tuple-element.31), kind=kOutput, calls=%fused_computation.2 | convolution fusion | flops 1612185600 | bytes 9699328 | tf_op jit(solution)/shard_map/dot_general | solution.py:253
  153.8 1.6 collective-permute-start.24
  155.3 7.9 %collective-permute-done.20 = bf16[128,2048]{1,0:T(8,128)(2,1)S(1)} collective-permute-done((bf16[128,2048]{1,0:T(8,128)(2,1)S(1)}, bf16[128,2048]{1,0:T(8,128)(2,1)S(1)}, u32[]{:S(2)}, u32[]{:S(2)}) %collective-permute-start.20) | collective-permute-done | bytes 524320 | tf_op jit(solution)/shard_map/ppermute | solution.py:215
  165.4 4.6 %fusion.44 = f32[2048,384]{1,0:T(8,128)S(1)} fusion(bf16[1024,2048]{1,0:T(8,128)(2,1)} %collective-permute-done.17, bf16[1024,384]{0,1:T(8,128)(2,1)S(1)} %get-tuple-element.20), kind=kOutput, calls=%fused_computation.103 | convolution fusion | flops 1610612736 | bytes 8126464 | tf_op jit(solution)/shard_map/dot_general | solution.py:253
  170.0 5.0 %collective-permute-done.21 = bf16[128,2048]{1,0:T(8,128)(2,1)S(1)} collective-permute-done((bf16[128,2048]{1,0:T(8,128)(2,1)S(1)}, bf16[128,2048]{1,0:T(8,128)(2,1)S(1)}, u32[]{:S(2)}, u32[]{:S(2)}) %collective-permute-start.21) | collective-permute-done | bytes 524320 | tf_op jit(solution)/shard_map/ppermute | solution.py:215
  176.9 3.6 %add_convert_fusion.3 = bf16[2048,384]{1,0:T(8,128)(2,1)} fusion(f32[2048,384]{1,0:T(8,128)S(1)} %fusion.44, bf16[1024,2048]{1,0:T(8,128)(2,1)S(1)} %copy-done.7, bf16[1024,384]{0,1:T(8,128)(2,1)S(1)} %get-tuple-element.22), kind=kOutput, calls=%fused_computation.3 | convolution fusion | flops 1612185600 | bytes 9699328 | tf_op jit(solution)/shard_map/dot_general | solution.py:253
  181.1 4.4 %all-to-all-start.1 = ((bf16[16,1,128]{2,1,0:T(2,128)(2,1)}), bf16[16,1,128]{2,1,0:T(2,128)(2,1)S(1)}, u32[]{:S(2)}, u32[]{:S(2)}) async-start(bf16[16,1,128]{2,1,0:T(2,128)(2,1)} %copy.26), calls=%async_computation.1 | async-start | bytes 16384 | tf_op jit(solution)/shard_map/all_to_all | solution.py:268
  185.5 2.1 constant_dynamic-slice_fusion.2
  188.1 3.8 %all-to-all-done.1 = bf16[16,1,128]{2,1,0:T(2,128)(2,1)S(1)} async-done(((bf16[16,1,128]{2,1,0:T(2,128)(2,1)}), bf16[16,1,128]{2,1,0:T(2,128)(2,1)S(1)}, u32[]{:S(2)}, u32[]{:S(2)}) %all-to-all-start.1) | async-done | bytes 4128 | tf_op jit(solution)/shard_map/all_to_all | solution.py:268
  192.5 2.3 %fusion.23 = bf16[1,1024,384]{2,1,0:T(8,128)(2,1)} fusion(bf16[1024,384]{1,0:T(8,128)(2,1)} %collective-permute-done.28, bf16[2048,384]{1,0:T(8,128)(2,1)S(1)} %add_convert_fusion.2, s32[]{:T(128)S(6)} %select_n.58), kind=kLoop, calls=%fused_computation.49 | loop fusion | flops 1572864 | bytes 2359300 | tf_op jit(solution)/shard_map/broadcast_in_dim | solution.py:263
  196.7 1.6 collective-permute-start.26
  198.3 9.5 %collective-permute-done.27 = bf16[1024,384]{1,0:T(8,128)(2,1)} collective-permute-done((bf16[1024,384]{1,0:T(8,128)(2,1)}, bf16[1024,384]{1,0:T(8,128)(2,1)}, u32[]{:S(2)}, u32[]{:S(2)}) %collective-permute-start.27) | collective-permute-done | bytes 786464 | tf_op jit(solution)/shard_map/ppermute | solution.py:137
  207.8 2.2 %fusion.22 = bf16[1,1024,384]{2,1,0:T(8,128)(2,1)} fusion(bf16[1024,384]{1,0:T(8,128)(2,1)} %collective-permute-done.27, bf16[2048,384]{1,0:T(8,128)(2,1)S(1)} %copy-done.4, s32[]{:T(128)S(6)} %select_n.58), kind=kLoop, calls=%fused_computation.48 | loop fusion | flops 1572864 | bytes 2359300 | tf_op jit(solution)/shard_map/broadcast_in_dim | solution.py:262
  210.0 2.4 %fusion.24 = bf16[1,192,2048]{2,1,0:T(8,128)(2,1)} fusion(bf16[192,2048]{1,0:T(8,128)(2,1)} %collective-permute-done.29, bf16[384,2048]{1,0:T(8,128)(2,1)S(1)} %add_convert_fusion.4, s32[]{:T(128)S(6)} %select_n.60), kind=kLoop, calls=%fused_computation.50 | loop fusion | flops 1572864 | bytes 2359300 | tf_op jit(solution)/shard_map/broadcast_in_dim | solution.py:267
  212.4 2.1 add_convert_fusion.8
  (105 shorter events, 31.9 us)
Async XLA Ops:
  0.6 96.8 %copy-start = (bf16[1,2048,384]{2,1,0:T(8,128)(2,1)S(1)}, bf16[1,2048,384]{2,1,0:T(8,128)(2,1)}, u32[]{:S(2)}) copy-start(bf16[1,2048,384]{2,1,0:T(8,128)(2,1)} %param.12) | copy-start | bytes 4718596
  0.6 30.0 %collective-permute-start.1 = (bf16[128,2048]{1,0:T(8,128)(2,1)}, bf16[128,2048]{1,0:T(8,128)(2,1)}, u32[]{:S(2)}, u32[]{:S(2)}) collective-permute-start(bf16[128,2048]{1,0:T(8,128)(2,1)} %param.8), channel_id=1, source_target_pairs={{0,4},{1,5},{4,8},{5,9},{8,12},{9,13},{12,14},{13,15},{14,10},{15,... | collective-permute-start | bytes 1572872 | tf_op jit(solution)/shard_map/ppermute | solution.py:181
  3.7 27.5 %collective-permute-start.9 = (bf16[128,2048]{1,0:T(8,128)(2,1)}, bf16[128,2048]{1,0:T(8,128)(2,1)S(1)}, u32[]{:S(2)}, u32[]{:S(2)}) collective-permute-start(bf16[128,2048]{1,0:T(8,128)(2,1)} %param.8), channel_id=1, source_target_pairs={{0,2},{1,3},{4,0},{5,1},{8,4},{9,5},{12,8},{13,9},{14,12},{15,13},... | collective-permute-start | bytes 1572872 | tf_op jit(solution)/shard_map/ppermute | solution.py:182
  3.7 30.8 %collective-permute-start = (bf16[128,2048]{1,0:T(8,128)(2,1)}, bf16[128,2048]{1,0:T(8,128)(2,1)S(1)}, u32[]{:S(2)}, u32[]{:S(2)}) collective-permute-start(bf16[128,2048]{1,0:T(8,128)(2,1)} %param.9), channel_id=1, source_target_pairs={{0,4},{1,5},{4,8},{5,9},{8,12},{9,13},{12,14},{13,15},{14,10},{15,... | collective-permute-start | bytes 1572872 | tf_op jit(solution)/shard_map/ppermute | solution.py:181
  5.8 29.4 %collective-permute-start.2 = (bf16[128,2048]{1,0:T(8,128)(2,1)}, bf16[128,2048]{1,0:T(8,128)(2,1)S(1)}, u32[]{:S(2)}, u32[]{:S(2)}) collective-permute-start(bf16[128,2048]{1,0:T(8,128)(2,1)} %param.9), channel_id=1, source_target_pairs={{0,2},{1,3},{4,0},{5,1},{8,4},{9,5},{12,8},{13,9},{14,12},{15,13},... | collective-permute-start | bytes 1572872 | tf_op jit(solution)/shard_map/ppermute | solution.py:182
  7.7 22.9 %all-to-all-start = ((bf16[16,1,128]{2,1,0:T(2,128)(2,1)}), bf16[16,1,128]{2,1,0:T(2,128)(2,1)S(1)}, u32[]{:S(2)}, u32[]{:S(2)}) async-start(bf16[16,1,128]{2,1,0:T(2,128)(2,1)} %copy.25), calls=%async_computation | async-start | bytes 16384 | tf_op jit(solution)/shard_map/all_to_all | solution.py:173
  30.6 15.0 %collective-permute-start.10 = (bf16[128,2048]{1,0:T(8,128)(2,1)}, bf16[128,2048]{1,0:T(8,128)(2,1)S(1)}, u32[]{:S(2)}, u32[]{:S(2)}) collective-permute-start(bf16[128,2048]{1,0:T(8,128)(2,1)} %collective-permute-done.1), channel_id=1, source_target_pairs={{0,4},{1,5},{4,8},{5,9},{8,12},{9,13},{12,14},{13,15},{14,10},{15,... | collective-permute-start | bytes 1572872 | tf_op jit(solution)/shard_map/ppermute | solution.py:181
  31.2 15.0 %collective-permute-start.11 = (bf16[128,2048]{1,0:T(8,128)(2,1)S(1)}, bf16[128,2048]{1,0:T(8,128)(2,1)S(1)}, u32[]{:S(2)}, u32[]{:S(2)}) collective-permute-start(bf16[128,2048]{1,0:T(8,128)(2,1)S(1)} %collective-permute-done.9), channel_id=1, source_target_pairs={{0,2},{1,3},{4,0},{5,1},{8,4},{9,5},{12,8},{13,9},{14,12},{15,13},... | collective-permute-start | bytes 1572872 | tf_op jit(solution)/shard_map/ppermute | solution.py:182
  34.6 22.3 %collective-permute-start.3 = (bf16[128,2048]{1,0:T(8,128)(2,1)S(1)}, bf16[128,2048]{1,0:T(8,128)(2,1)S(1)}, u32[]{:S(2)}, u32[]{:S(2)}) collective-permute-start(bf16[128,2048]{1,0:T(8,128)(2,1)S(1)} %collective-permute-done), channel_id=1, source_target_pairs={{0,4},{1,5},{4,8},{5,9},{8,12},{9,13},{12,14},{13,15},{14,10},{15,... | collective-permute-start | bytes 1572872 | tf_op jit(solution)/shard_map/ppermute | solution.py:181
  35.1 22.3 %collective-permute-start.4 = (bf16[128,2048]{1,0:T(8,128)(2,1)S(1)}, bf16[128,2048]{1,0:T(8,128)(2,1)S(1)}, u32[]{:S(2)}, u32[]{:S(2)}) collective-permute-start(bf16[128,2048]{1,0:T(8,128)(2,1)S(1)} %collective-permute-done.2), channel_id=1, source_target_pairs={{0,2},{1,3},{4,0},{5,1},{8,4},{9,5},{12,8},{13,9},{14,12},{15,13},... | collective-permute-start | bytes 1572872 | tf_op jit(solution)/shard_map/ppermute | solution.py:182
  45.7 22.5 %collective-permute-start.12 = (bf16[128,2048]{1,0:T(8,128)(2,1)S(1)}, bf16[128,2048]{1,0:T(8,128)(2,1)S(1)}, u32[]{:S(2)}, u32[]{:S(2)}) collective-permute-start(bf16[128,2048]{1,0:T(8,128)(2,1)S(1)} %collective-permute-done.10), channel_id=1, source_target_pairs={{0,4},{1,5},{4,8},{5,9},{8,12},{9,13},{12,14},{13,15},{14,10},{15,... | collective-permute-start | bytes 1572872 | tf_op jit(solution)/shard_map/ppermute | solution.py:181
  46.2 22.5 %collective-permute-start.13 = (bf16[128,2048]{1,0:T(8,128)(2,1)S(1)}, bf16[128,2048]{1,0:T(8,128)(2,1)S(1)}, u32[]{:S(2)}, u32[]{:S(2)}) collective-permute-start(bf16[128,2048]{1,0:T(8,128)(2,1)S(1)} %collective-permute-done.11), channel_id=1, source_target_pairs={{0,2},{1,3},{4,0},{5,1},{8,4},{9,5},{12,8},{13,9},{14,12},{15,13},... | collective-permute-start | bytes 1572872 | tf_op jit(solution)/shard_map/ppermute | solution.py:182
  56.9 29.6 %collective-permute-start.5 = (bf16[128,2048]{1,0:T(8,128)(2,1)S(1)}, bf16[128,2048]{1,0:T(8,128)(2,1)S(1)}, u32[]{:S(2)}, u32[]{:S(2)}) collective-permute-start(bf16[128,2048]{1,0:T(8,128)(2,1)S(1)} %collective-permute-done.3), channel_id=1, source_target_pairs={{0,4},{1,5},{4,8},{5,9},{8,12},{9,13},{12,14},{13,15},{14,10},{15,... | collective-permute-start | bytes 1572872 | tf_op jit(solution)/shard_map/ppermute | solution.py:181
  57.5 30.0 %collective-permute-start.6 = (bf16[128,2048]{1,0:T(8,128)(2,1)S(1)}, bf16[128,2048]{1,0:T(8,128)(2,1)S(1)}, u32[]{:S(2)}, u32[]{:S(2)}) collective-permute-start(bf16[128,2048]{1,0:T(8,128)(2,1)S(1)} %collective-permute-done.4), channel_id=1, source_target_pairs={{0,2},{1,3},{4,0},{5,1},{8,4},{9,5},{12,8},{13,9},{14,12},{15,13},... | collective-permute-start | bytes 1572872 | tf_op jit(solution)/shard_map/ppermute | solution.py:182
  68.1 15.7 %collective-permute-start.14 = (bf16[128,1024]{1,0:T(8,128)(2,1)S(1)}, bf16[128,1024]{1,0:T(8,128)(2,1)S(1)}, u32[]{:S(2)}, u32[]{:S(2)}) collective-permute-start(bf16[128,1024]{1,0:T(8,128)(2,1)S(1)} %slice.72), channel_id=1, source_target_pairs={{0,4},{1,5},{4,8},{5,9},{8,12},{9,13},{12,14},{13,15},{14,10},{15,... | collective-permute-start | bytes 786440 | tf_op jit(solution)/shard_map/ppermute | solution.py:189
  68.8 15.1 %collective-permute-start.15 = (bf16[128,1024]{1,0:T(8,128)(2,1)S(1)}, bf16[128,1024]{1,0:T(8,128)(2,1)S(1)}, u32[]{:S(2)}, u32[]{:S(2)}) collective-permute-start(bf16[128,1024]{1,0:T(8,128)(2,1)S(1)} %slice.73), channel_id=1, source_target_pairs={{0,2},{1,3},{4,0},{5,1},{8,4},{9,5},{12,8},{13,9},{14,12},{15,13},... | collective-permute-start | bytes 786440 | tf_op jit(solution)/shard_map/ppermute | solution.py:190
  84.8 12.6 %collective-permute-start.17 = (bf16[1024,2048]{1,0:T(8,128)(2,1)}, bf16[1024,2048]{1,0:T(8,128)(2,1)}, u32[]{:S(2)}, u32[]{:S(2)}) collective-permute-start(bf16[1024,2048]{1,0:T(8,128)(2,1)} %maximum_dynamic-update-slice_fusion.1), channel_id=1, source_target_pairs={{0,1},{1,0},{2,3},{3,2},{4,5},{5,4},{6,7},{7,6},{8,9},{9,8},{10,11... | collective-permute-start | bytes 12582920 | tf_op jit(solution)/shard_map/ppermute | solution.py:196
  86.5 8.8 %collective-permute-start.7 = (bf16[128,1024]{1,0:T(8,128)(2,1)S(1)}, bf16[128,1024]{1,0:T(8,128)(2,1)S(1)}, u32[]{:S(2)}, u32[]{:S(2)}) collective-permute-start(bf16[128,1024]{1,0:T(8,128)(2,1)S(1)} %slice.70), channel_id=1, source_target_pairs={{0,4},{1,5},{4,8},{5,9},{8,12},{9,13},{12,14},{13,15},{14,10},{15,... | collective-permute-start | bytes 786440 | tf_op jit(solution)/shard_map/ppermute | solution.py:189
  87.5 9.6 %copy-start.9 = (s32[8]{0:T(128)S(1)}, s32[8]{0:T(128)}, u32[]{:S(2)}) copy-start(s32[8]{0:T(128)} %constant.79.clone) | copy-start | bytes 100
  87.5 8.7 %collective-permute-start.8 = (bf16[128,1024]{1,0:T(8,128)(2,1)S(1)}, bf16[128,1024]{1,0:T(8,128)(2,1)S(1)}, u32[]{:S(2)}, u32[]{:S(2)}) collective-permute-start(bf16[128,1024]{1,0:T(8,128)(2,1)S(1)} %slice.71), channel_id=1, source_target_pairs={{0,2},{1,3},{4,0},{5,1},{8,4},{9,5},{12,8},{13,9},{14,12},{15,13},... | collective-permute-start | bytes 786440 | tf_op jit(solution)/shard_map/ppermute | solution.py:190
  97.0 8.7 %collective-permute-start.16 = (bf16[1024,2048]{1,0:T(8,128)(2,1)}, bf16[1024,2048]{1,0:T(8,128)(2,1)}, u32[]{:S(2)}, u32[]{:S(2)}) collective-permute-start(bf16[1024,2048]{1,0:T(8,128)(2,1)} %maximum_dynamic-update-slice_fusion), channel_id=1, source_target_pairs={{0,1},{1,0},{2,3},{3,2},{4,5},{5,4},{6,7},{7,6},{8,9},{9,8},{10,11... | collective-permute-start | bytes 12582920 | tf_op jit(solution)/shard_map/ppermute | solution.py:196
  97.4 4.2 %copy-start.3 = (bf16[1,2048,384]{2,1,0:T(8,128)(2,1)S(1)}, bf16[1,2048,384]{2,1,0:T(8,128)(2,1)}, u32[]{:S(2)}) copy-start(bf16[1,2048,384]{2,1,0:T(8,128)(2,1)} %param.13) | copy-start | bytes 4718596
  101.6 4.2 %copy-start.10 = (bf16[1,384,2048]{2,1,0:T(8,128)(2,1)S(1)}, bf16[1,384,2048]{2,1,0:T(8,128)(2,1)}, u32[]{:S(2)}) copy-start(bf16[1,384,2048]{2,1,0:T(8,128)(2,1)} %param.14) | copy-start | bytes 4718596
  105.7 5.2 %copy-start.11 = (f32[1024,384]{0,1:T(8,128)}, f32[1024,384]{0,1:T(8,128)S(1)}, u32[]{:S(2)}) copy-start(f32[1024,384]{0,1:T(8,128)S(1)} %fusion.9) | copy-start | bytes 4718596
  113.3 3.0 %copy-start.6 = (bf16[1024,2048]{1,0:T(8,128)(2,1)S(1)}, bf16[1024,2048]{1,0:T(8,128)(2,1)}, u32[]{:S(2)}) copy-start(bf16[1024,2048]{1,0:T(8,128)(2,1)} %maximum_dynamic-update-slice_fusion.1) | copy-start | bytes 12582916
  115.7 22.9 %collective-permute-start.18 = (bf16[1024,2048]{1,0:T(8,128)(2,1)S(1)}, bf16[1024,2048]{1,0:T(8,128)(2,1)S(1)}, u32[]{:S(2)}, u32[]{:S(2)}) collective-permute-start(bf16[1024,2048]{1,0:T(8,128)(2,1)S(1)} %add_convert_fusion.1), channel_id=1, source_target_pairs={{0,1},{1,0},{2,3},{3,2},{4,5},{5,4},{6,7},{7,6},{8,9},{9,8},{10,11... | collective-permute-start | bytes 12582920 | tf_op jit(solution)/shard_map/ppermute | solution.py:246
  125.4 2.7 %copy-start.12 = (f32[1024,384]{0,1:T(8,128)S(1)}, f32[1024,384]{0,1:T(8,128)}, u32[]{:S(2)}) copy-start(f32[1024,384]{0,1:T(8,128)} %copy-done.11) | copy-start | bytes 4718596
  137.1 72.9 %collective-permute-start.29 = (bf16[192,2048]{1,0:T(8,128)(2,1)}, bf16[192,2048]{1,0:T(8,128)(2,1)}, u32[]{:S(2)}, u32[]{:S(2)}) collective-permute-start(bf16[192,2048]{1,0:T(8,128)(2,1)} %constant_dynamic-slice_fusion), channel_id=1, source_target_pairs={{0,16},{16,0},{1,17},{17,1},{2,18},{18,2},{3,19},{19,3},{4,20},{20... | collective-permute-start | bytes 2359304 | tf_op jit(solution)/shard_map/ppermute | solution.py:137
  141.1 33.9 %copy-start.2 = (bf16[1024,2048]{1,0:T(8,128)(2,1)}, bf16[1024,2048]{1,0:T(8,128)(2,1)S(1)}, u32[]{:S(2)}) copy-start(bf16[1024,2048]{1,0:T(8,128)(2,1)S(1)} %add_convert_fusion) | copy-start | bytes 12582916
  141.2 8.0 %collective-permute-start.19 = (bf16[128,1024]{1,0:T(8,128)(2,1)S(1)}, bf16[128,1024]{1,0:T(8,128)(2,1)S(1)}, u32[]{:S(2)}, u32[]{:S(2)}) collective-permute-start(bf16[128,1024]{1,0:T(8,128)(2,1)S(1)} %get-tuple-element.27), channel_id=1, source_target_pairs={{0,4},{1,5},{4,8},{5,9},{8,12},{9,13},{12,14},{13,15},{14,10},{15,... | collective-permute-start | bytes 786440 | tf_op jit(solution)/shard_map/ppermute | solution.py:206
  142.7 7.8 %collective-permute-start.23 = (bf16[128,1024]{1,0:T(8,128)(2,1)S(1)}, bf16[128,1024]{1,0:T(8,128)(2,1)S(1)}, u32[]{:S(2)}, u32[]{:S(2)}) collective-permute-start(bf16[128,1024]{1,0:T(8,128)(2,1)S(1)} %get-tuple-element.28), channel_id=1, source_target_pairs={{0,2},{1,3},{4,0},{5,1},{8,4},{9,5},{12,8},{13,9},{14,12},{15,13},... | collective-permute-start | bytes 786440 | tf_op jit(solution)/shard_map/ppermute | solution.py:207
  143.4 7.9 %copy-start.7 = (bf16[1024,2048]{1,0:T(8,128)(2,1)S(1)}, bf16[1024,2048]{1,0:T(8,128)(2,1)}, u32[]{:S(2)}) copy-start(bf16[1024,2048]{1,0:T(8,128)(2,1)} %maximum_dynamic-update-slice_fusion.1) | copy-start | bytes 12582916
  150.8 12.5 %collective-permute-start.20 = (bf16[128,2048]{1,0:T(8,128)(2,1)S(1)}, bf16[128,2048]{1,0:T(8,128)(2,1)S(1)}, u32[]{:S(2)}, u32[]{:S(2)}) collective-permute-start(bf16[128,2048]{1,0:T(8,128)(2,1)S(1)} %pad_maximum_fusion), channel_id=1, source_target_pairs={{0,4},{1,5},{4,8},{5,9},{8,12},{9,13},{12,14},{13,15},{14,10},{15,... | collective-permute-start | bytes 1572872 | tf_op jit(solution)/shard_map/ppermute | solution.py:215
  153.8 16.3 %collective-permute-start.24 = (bf16[128,2048]{1,0:T(8,128)(2,1)S(1)}, bf16[128,2048]{1,0:T(8,128)(2,1)S(1)}, u32[]{:S(2)}, u32[]{:S(2)}) collective-permute-start(bf16[128,2048]{1,0:T(8,128)(2,1)S(1)} %pad_maximum_fusion.1), channel_id=1, source_target_pairs={{0,2},{1,3},{4,0},{5,1},{8,4},{9,5},{12,8},{13,9},{14,12},{15,13},... | collective-permute-start | bytes 1572872 | tf_op jit(solution)/shard_map/ppermute | solution.py:216
  163.4 11.6 %collective-permute-start.21 = (bf16[128,2048]{1,0:T(8,128)(2,1)S(1)}, bf16[128,2048]{1,0:T(8,128)(2,1)S(1)}, u32[]{:S(2)}, u32[]{:S(2)}) collective-permute-start(bf16[128,2048]{1,0:T(8,128)(2,1)S(1)} %add_convert_fusion.12), channel_id=1, source_target_pairs={{0,4},{1,5},{4,8},{5,9},{8,12},{9,13},{12,14},{13,15},{14,10},{15,... | collective-permute-start | bytes 1572872 | tf_op jit(solution)/shard_map/ppermute | solution.py:215
  164.9 27.6 %collective-permute-start.28 = (bf16[1024,384]{1,0:T(8,128)(2,1)}, bf16[1024,384]{1,0:T(8,128)(2,1)}, u32[]{:S(2)}, u32[]{:S(2)}) collective-permute-start(bf16[1024,384]{1,0:T(8,128)(2,1)} %constant_dynamic-slice_fusion.1), channel_id=1, source_target_pairs={{0,16},{16,0},{1,17},{17,1},{2,18},{18,2},{3,19},{19,3},{4,20},{20... | collective-permute-start | bytes 2359304 | tf_op jit(solution)/shard_map/ppermute | solution.py:137
  176.4 19.0 %collective-permute-start.25 = (bf16[128,2048]{1,0:T(8,128)(2,1)}, bf16[128,2048]{1,0:T(8,128)(2,1)}, u32[]{:S(2)}, u32[]{:S(2)}) collective-permute-start(bf16[128,2048]{1,0:T(8,128)(2,1)} %get-tuple-element.24), channel_id=1, source_target_pairs={{0,2},{1,3},{4,0},{5,1},{8,4},{9,5},{12,8},{13,9},{14,12},{15,13},... | collective-permute-start | bytes 1572872 | tf_op jit(solution)/shard_map/ppermute | solution.py:216
  180.5 11.4 %copy-start.8 = (s32[128,4]{0,1:T(4,128)S(1)}, s32[128,4]{0,1:T(4,128)}, u32[]{:S(2)}) copy-start(s32[128,4]{0,1:T(4,128)} %param.10) | copy-start | bytes 6148
  181.1 10.8 %all-to-all-start.1 = ((bf16[16,1,128]{2,1,0:T(2,128)(2,1)}), bf16[16,1,128]{2,1,0:T(2,128)(2,1)S(1)}, u32[]{:S(2)}, u32[]{:S(2)}) async-start(bf16[16,1,128]{2,1,0:T(2,128)(2,1)} %copy.26), calls=%async_computation.1 | async-start | bytes 16384 | tf_op jit(solution)/shard_map/all_to_all | solution.py:268
  187.6 20.2 %collective-permute-start.27 = (bf16[1024,384]{1,0:T(8,128)(2,1)}, bf16[1024,384]{1,0:T(8,128)(2,1)}, u32[]{:S(2)}, u32[]{:S(2)}) collective-permute-start(bf16[1024,384]{1,0:T(8,128)(2,1)} %constant_dynamic-slice_fusion.2), channel_id=1, source_target_pairs={{0,16},{16,0},{1,17},{17,1},{2,18},{18,2},{3,19},{19,3},{4,20},{20... | collective-permute-start | bytes 2359304 | tf_op jit(solution)/shard_map/ppermute | solution.py:137
  191.9 2.9 %copy-start.5 = (bf16[128,2048]{1,0:T(8,128)(2,1)S(1)}, bf16[128,2048]{1,0:T(8,128)(2,1)}, u32[]{:S(2)}) copy-start(bf16[128,2048]{1,0:T(8,128)(2,1)} %get-tuple-element.23) | copy-start | bytes 1572868
  192.5 15.3 %copy-start.4 = (bf16[2048,384]{1,0:T(8,128)(2,1)S(1)}, bf16[2048,384]{1,0:T(8,128)(2,1)}, u32[]{:S(2)}) copy-start(bf16[2048,384]{1,0:T(8,128)(2,1)} %add_convert_fusion.3) | copy-start | bytes 4718596
  194.9 17.6 %collective-permute-start.22 = (bf16[128,2048]{1,0:T(8,128)(2,1)S(1)}, bf16[128,2048]{1,0:T(8,128)(2,1)S(1)}, u32[]{:S(2)}, u32[]{:S(2)}) collective-permute-start(bf16[128,2048]{1,0:T(8,128)(2,1)S(1)} %copy-done.5), channel_id=1, source_target_pairs={{0,4},{1,5},{4,8},{5,9},{8,12},{9,13},{12,14},{13,15},{14,10},{15,... | collective-permute-start | bytes 1572872 | tf_op jit(solution)/shard_map/ppermute | solution.py:215
  196.7 15.7 %collective-permute-start.26 = (bf16[128,2048]{1,0:T(8,128)(2,1)S(1)}, bf16[128,2048]{1,0:T(8,128)(2,1)S(1)}, u32[]{:S(2)}, u32[]{:S(2)}) collective-permute-start(bf16[128,2048]{1,0:T(8,128)(2,1)S(1)} %add_convert_fusion.9), channel_id=1, source_target_pairs={{0,2},{1,3},{4,0},{5,1},{8,4},{9,5},{12,8},{13,9},{14,12},{15,13},... | collective-permute-start | bytes 1572872 | tf_op jit(solution)/shard_map/ppermute | solution.py:216
  210.0 4.5 %copy-start.1 = (bf16[1,2048,384]{2,1,0:T(8,128)(2,1)S(1)}, bf16[1,2048,384]{2,1,0:T(8,128)(2,1)}, u32[]{:S(2)}) copy-start(bf16[1,2048,384]{2,1,0:T(8,128)(2,1)} %param.12) | copy-start | bytes 4718596
